TPU v7x, 32 devices: a whole 2x2x4 slice. The times are simulated.
32 devices in a mesh: blk: 16 (over z, y, core), cls: 2 (over x).
Axes of the slice: x: 2, y: 2, z: 4, core: 2. Of those that a mesh axis runs over, the one named last changes fastest.
Arguments:
- features: bfloat16 [1024, 2048], P('blk'), may hold values from -6 to 6
- labels: int32 [1024], P('blk'), may hold values from 0 to 655359
- offset: int32 [1], replicated, may hold values from 0 to 524288
- other_lse: float32 [1024], replicated, may hold values from 15 to 20
- weight: bfloat16 [131072, 2048], P(('blk', 'cls'))
- accum: float32 [131072, 2048], P(('blk', 'cls')), may hold values from 0.1 to 1
Outputs:
- new_weight: bfloat16 [131072, 2048], P(('blk', 'cls'))
- new_accum: float32 [131072, 2048], P(('blk', 'cls'))
- lse: float32 [1024], P('blk')
All inputs are finite; a program needn't handle non-finite values.
Results may differ from a plain program's by a relative error of at most 0.004.
Values may be sent and summed in bfloat16 or wider, within the bound.
No kernel may reach another device: no remote copies, remote signals or barrier semaphores. Data moves between devices by JAX's collectives and lax.ppermute only.
A program may use at most 192 MiB of HBM per device.

v0:
```python
import jax
import jax.numpy as jnp
from jax import lax
from jax.sharding import PartitionSpec as P


def scores(rows, weight):
    return lax.dot_general(
        rows, weight, (((1,), (1,)), ((), ())), preferred_element_type=jnp.float32
    )


def gradient_term(logits, lse_rows, label_rows, first_class, rows):
    width = logits.shape[1]
    local = label_rows - first_class
    onehot = (local[:, None] == jnp.arange(width, dtype=jnp.int32)[None, :]).astype(jnp.float32)
    delta = (jnp.exp(logits - lse_rows[:, None]) - onehot).astype(jnp.bfloat16)
    return lax.dot_general(
        delta, rows, (((0,), (0,)), ((), ())), preferred_element_type=jnp.float32
    )


def body(features, labels, offset, other_lse, weight, accum):
    block = features.shape[0]
    cls_dev = weight.shape[0]
    device_rank = lax.axis_index("blk") * lax.axis_size("cls") + lax.axis_index("cls")
    first_class = offset[0] + device_rank * cls_dev
    all_rows, all_labels = (
        lax.all_gather(features, "blk", axis=0, tiled=True),
        lax.all_gather(labels, "blk", axis=0, tiled=True),
    )
    logits = scores(all_rows, weight)
    local_top = jnp.max(logits, axis=1)
    top = lax.pmax(local_top, ("blk", "cls"))
    total = lax.psum(jnp.sum(jnp.exp(logits - top[:, None]), axis=1), ("blk", "cls"))
    slab_lse = top + jnp.log(total)
    high = jnp.maximum(slab_lse, other_lse)
    lse = high + jnp.log(jnp.exp(slab_lse - high) + jnp.exp(other_lse - high))
    grad = gradient_term(logits, lse, all_labels, first_class, all_rows)
    new_accum = accum + grad * grad
    new_weight = (weight.astype(jnp.float32) - 0.05 * grad / (jnp.sqrt(new_accum) + 1e-10)).astype(
        jnp.bfloat16
    )
    own_lse = lax.dynamic_slice_in_dim(lse, lax.axis_index("blk") * block, block, 0)
    return (new_weight, new_accum, own_lse)


def solution(mesh):
    in_specs = (
        P("blk", None),
        P("blk"),
        P(),
        P(),
        P(("blk", "cls"), None),
        P(("blk", "cls"), None),
    )
    out_specs = (P(("blk", "cls"), None), P(("blk", "cls"), None), P("blk"))
    return jax.shard_map(body, mesh=mesh, in_specs=in_specs, out_specs=out_specs, check_vma=False)
```

profile of v0, /device:TPU:0, one launch (start us, length us, event | category | flops | bytes accessed | tf_op | source)
XLA Modules:
  0.0 232.0 jit_solution(12426884175506996775)
XLA Ops:
  7.2 0.0 all-gather.2.cloned.1.call-start
  7.2 0.7 all-gather.2.cloned.1.call-update
  8.6 1.2 dynamic-slice
  10.5 0.9 dynamic-update-slice
  11.3 13.8 %all-reduce = s32[1024]{0:T(1024)S(1)} all-reduce(s32[1024]{0:T(1024)S(1)} %dynamic-update-slice), channel_id=1, replica_groups=mesh['blk'=16,'cls'=2] {'blk'}, use_global_device_ids=true, to_apply=%add | all-reduce | flops 1024 | bytes 8192
  25.1 38.3 %all-gather.2.cloned.1.call-done = bf16[1024,2048]{1,0:T(8,128)(2,1)} async-done(((bf16[64,2048]{1,0:T(8,128)(2,1)}), bf16[1024,2048]{1,0:T(8,128)(2,1)}) %all-gather.2.cloned.1.call-update) | async-done | bytes 4194320 | tf_op jit(solution)/shard_map/all_gather | solution.py:29
  63.5 23.8 %fusion.4 = (f32[1024]{0:T(1024)S(1)}, f32[1024,4096]{1,0:T(8,128)}) fusion(bf16[1024,2048]{1,0:T(8,128)(2,1)} %all-gather.2.cloned.1.call-done, bf16[4096,2048]{1,0:T(8,128)(2,1)} %param.10), kind=kOutput, calls=%fused_computation.12 | convolution fusion | flops 17184063488 | bytes 37752832 | tf_op jit(solution)/shard_map/dot_general | solution.py:8
  87.3 0.0 copy-start
  87.3 39.2 %pmax.7 = f32[1024]{0:T(1024)S(1)} all-reduce(f32[1024]{0:T(1024)S(1)} %get-tuple-element.5), channel_id=1, replica_groups=mesh['blk'=16,'cls'=2] {'blk','cls'}, use_global_device_ids=true, to_apply=%region_1.0 | all-reduce | flops 1024 | bytes 8192 | tf_op jit(solution)/shard_map/pmax | solution.py:34
  126.5 8.1 %exponential_reduce_fusion = f32[1024]{0:T(1024)S(1)} fusion(f32[1024,4096]{1,0:T(8,128)} %get-tuple-element.6, f32[1024]{0:T(1024)S(1)} %pmax.7), kind=kLoop, calls=%fused_computation.4 | loop fusion | flops 8387584 | bytes 16785408 | tf_op jit(solution)/shard_map/reduce_sum | solution.py:35
  134.6 40.2 %psum.7 = f32[1024]{0:T(1024)S(1)} all-reduce(f32[1024]{0:T(1024)S(1)} %exponential_reduce_fusion), channel_id=1, replica_groups=mesh['blk'=16,'cls'=2] {'blk','cls'}, use_global_device_ids=true, to_apply=%region_3.0 | all-reduce | flops 1024 | bytes 8192 | tf_op jit(solution)/shard_map/psum | solution.py:35
  174.8 0.0 copy-done
  174.8 0.6 dynamic_slice.3
  175.4 49.7 %subtract_convert_fusion = (bf16[4096,2048]{1,0:T(8,128)(2,1)}, f32[4096,2048]{1,0:T(8,128)}) fusion(bf16[4096,2048]{1,0:T(8,128)(2,1)} %param.10, f32[4096,2048]{1,0:T(8,128)} %param.11, bf16[1024,2048]{1,0:T(8,128)(2,1)} %all-gather.2.cloned.1.call-done, f32[1024,4096]{1,0:T(8,128)} %get-tuple-element.6, s32[1024]{0:T(1024)S(1)} %broadcast_subtract_fusion, ...), kind=kOutput, calls=%fused_computation | convolution fusion | flops 17267949568 | bytes 121643008 | tf_op jit(solution)/shard_map/dot_general | solution.py:18
  (3 shorter events, 0.0 us)
Async XLA Ops:
  7.2 56.3 %all-gather.2.cloned.1.call-start = ((), (), s32[]{:S(2)}) async-start(), calls=%async_computation | async-start | bytes 4456448 | tf_op jit(solution)/shard_map/all_gather | solution.py:29
  87.3 87.5 %copy-start = (f32[1024]{0:T(1024)S(1)}, f32[1024]{0:T(1024)}, u32[]{:S(2)}) copy-start(f32[1024]{0:T(1024)} %param.9) | copy-start | bytes 12292
Sparse Core Ops, SparseCore 0:
  10.2 53.2 all-gather.1
where the time goes:
time: 232 us
  blocking collectives  93.2 us (40%)
  matrix products  73.5 us (32%)
  waiting for transfers between devices  39 us (17%)
  between operations  15.3 us (7%)
  other arithmetic  8.11 us (3%)
  local copies, waits for them, and re-layouts  2.71 us (1%)
    dot_general x1, matrix products, gradient_term(): lax.dot_general(delta, rows, (((0,), (0,)), ((), ())), preferred_element_...  49.7 us
    psum x1, blocking collectives, body(): lax.psum(jnp.sum(jnp.exp(logits - top[:, None]), axis=1), ('blk', 'cls'))  40.2 us
    pmax x1, blocking collectives, body(): top = lax.pmax(local_top, ('blk', 'cls'))  39.2 us
    all_gather x1, waiting for transfers between devices, body(): lax.all_gather(features, 'blk', axis=0, tiled=True)  38.3 us
    dot_general x1, matrix products, scores(): lax.dot_general(rows, weight, (((1,), (1,)), ((), ())), preferred_element...  23.8 us
    unnamed x1, blocking collectives  13.8 us
    reduce_sum x1, other arithmetic, body(): jnp.sum(jnp.exp(logits - top[:, None]), axis=1)  8.09 us
  transfers between devices with their start and end apart: 1, of which 1 were waited for; matrix products, arithmetic and copies ran while one was open for 1% of the time, Pallas kernels for 0%

commit v1 on v0

v1 whole, which is shorter than its diff:
```python
import functools

import jax
import jax.numpy as jnp
from jax import lax
from jax.experimental import pallas as pl
from jax.experimental.pallas import tpu as pltpu
from jax.sharding import PartitionSpec as P

f32, bf16, i32 = jnp.float32, jnp.bfloat16, jnp.int32
VM = pl.BlockSpec(memory_space=pltpu.VMEM)
ANY = pl.BlockSpec(memory_space=pl.ANY)
SM = pl.BlockSpec(memory_space=pltpu.SMEM)
MIB = 2**20
LANES = 128
HELD_BYTES = 16 * MIB
LAG = 2
NO_LABEL = -4.0e6
SCOPED = 4 * MIB


def in_vmem(x):
    return pltpu.with_memory_space_constraint(x, pltpu.VMEM)


def in_hbm(x):
    return pltpu.with_memory_space_constraint(x, pltpu.HBM)


def ring_chips(chips):
    half = chips // 2
    return [2 * p if p < half else 2 * (chips - 1 - p) + 1 for p in range(chips)]


def ring_pairs(chips):
    ring = ring_chips(chips)
    pairs = []
    for p in range(chips):
        pairs.append((2 * ring[p], 2 * ring[(p + 1) % chips]))
        pairs.append((2 * ring[p] + 1, 2 * ring[p - 1] + 1))
    return pairs


def chip_at(place, chips):
    place = lax.rem(place + 2 * chips, chips)
    return jnp.where(place < chips // 2, 2 * place, 2 * (chips - 1 - place) + 1)


def whereabouts(chips):
    blk = lax.axis_index("blk")
    chip, core = blk // 2, lax.rem(blk, 2)
    z = chip // 2
    place = jnp.where(lax.rem(chip, 2) == 0, z, chips - 1 - z)
    return chip, core, place


def pair_slots(chips):
    _, core, place = whereabouts(chips)
    sign = 1 - 2 * core
    slots = [(chip_at(place, chips), core)]
    for step in range(1, chips // 2):
        slots.append((chip_at(place - step * sign, chips), core))
        slots.append((chip_at(place + step * sign, chips), 1 - core))
    slots.append((chip_at(place + chips // 2, chips), core))
    return slots


def swapped(row, swap):
    half = row.shape[1] // 2
    other = jnp.concatenate([row[:, half:], row[:, :half]], axis=1)
    return jnp.where(swap == 1, other, row)


def merge_parts(messages):
    n = messages[0].shape[0] // 3
    tops = [m[:n] for m in messages]
    top = functools.reduce(jnp.maximum, tops)
    total = sum(m[n : 2 * n] * jnp.exp(t - top) for m, t in zip(messages, tops))
    return top, total, functools.reduce(jnp.maximum, [m[2 * n :] for m in messages])


def hold_kernel(chips, pieces, w_hbm, pair_hbm, labels_hbm, offset_ref, *refs):
    w_ref, _, x_ref, _, msg_ref, labels_ref, sem, pair_sem, label_sem = refs
    rows = w_ref.shape[0] // pieces
    copies = [
        pltpu.make_async_copy(
            w_hbm.at[pl.ds(i * rows, rows)], w_ref.at[pl.ds(i * rows, rows)], sem.at[i]
        )
        for i in range(pieces)
    ]
    label_copy = pltpu.make_async_copy(labels_hbm, labels_ref, label_sem)
    label_copy.start()
    pair_copy = pltpu.make_async_copy(
        pair_hbm, x_ref.at[pl.ds(0, pair_hbm.shape[0])], pair_sem
    )
    pair_copy.start()
    for copy in copies:
        copy.start()
    label_copy.wait()
    msg_ref[: 2 * chips] = jnp.zeros((2 * chips, LANES), f32)
    msg_ref[2 * chips :] = jnp.full((chips, LANES), NO_LABEL, f32)
    mine = (labels_ref[...] - offset_ref[0]).astype(f32)
    none = jnp.full_like(mine, NO_LABEL)
    chip, core, _ = whereabouts(chips)
    msg_ref[pl.ds(2 * chips + chip, 1), :] = jnp.concatenate(
        [jnp.where(core == 0, mine, none), jnp.where(core == 0, none, mine)], axis=1
    )
    for copy in copies:
        copy.wait()
    pair_copy.wait()


def hold(weight, pair, labels, offset, chips, batch, held_rows):
    pieces = 4
    rows, feats = weight.shape
    labels = labels.reshape(1, -1)
    return pl.pallas_call(
        functools.partial(hold_kernel, chips, pieces),
        name="hold_weight",
        out_shape=[
            pltpu.VMEM((rows, feats), bf16),
            pltpu.VMEM((rows, batch), f32),
            pltpu.VMEM((batch, feats), bf16),
            pltpu.VMEM((held_rows, feats), f32),
            pltpu.VMEM((3 * chips, LANES), f32),
        ],
        in_specs=[ANY, ANY, ANY, SM],
        out_specs=[VM] * 5,
        scratch_shapes=[
            pltpu.VMEM(labels.shape, i32),
            pltpu.SemaphoreType.DMA((pieces,)),
            pltpu.SemaphoreType.DMA,
            pltpu.SemaphoreType.DMA,
        ],
        compiler_params=pltpu.CompilerParams(vmem_limit_bytes=SCOPED),
        cost_estimate=pl.CostEstimate(
            flops=0, bytes_accessed=weight.size * 2, transcendentals=0
        ),
    )(in_hbm(weight), in_hbm(pair), in_hbm(labels), offset)


def fold(op, values):
    return op(values.reshape(values.shape[0] // 8, 8, values.shape[1]), axis=0)


def more_stats(logits, top, total):
    new_top = jnp.maximum(top, fold(jnp.max, logits))
    terms = jnp.exp(logits.reshape(logits.shape[0] // 8, 8, logits.shape[1]) - new_top[None])
    return new_top, total * jnp.exp(top - new_top) + jnp.sum(terms, axis=0)


def score_kernel(cfg, *refs):
    chips, k, held, bm, n_blocks = cfg
    blocks, accum_hbm, refs = refs[:n_blocks], refs[n_blocks], refs[n_blocks + 1 :]
    msg_in, refs = refs[0], refs[5:]
    msg_ref, w_ref, logits_ref, x_ref, acc_ref, acc_sem, x_sem = refs
    rows, width = w_ref.shape[0], 2 * LANES
    columns = pl.ds(k * width, width)
    accum_copy = None
    if held[1] > held[0]:
        part = pl.ds(held[0], held[1] - held[0])
        accum_copy = pltpu.make_async_copy(accum_hbm.at[part], acc_ref.at[part], acc_sem)
        accum_copy.start()
    if k == 0:
        copy = pltpu.make_async_copy(blocks[0], x_ref.at[pl.ds(LANES, LANES)], x_sem)
        copy.start()
        copy.wait()
    else:
        at = k * width
        for block in blocks:
            x_ref[pl.ds(at, block.shape[0]), :] = block[...]
            at += block.shape[0]
    x = x_ref.at[columns]
    top = jnp.full((8, width), -3.0e38, f32)
    total = jnp.zeros((8, width), f32)
    for i in range(rows // bm):
        logits_ref[pl.ds(i * bm, bm), columns] = lax.dot_general(
            w_ref[pl.ds(i * bm, bm), :],
            x[...],
            (((1,), (1,)), ((), ())),
            preferred_element_type=f32,
        )
        if i > 0:
            top, total = more_stats(logits_ref[pl.ds((i - 1) * bm, bm), columns], top, total)
    top, total = more_stats(logits_ref[pl.ds(rows - bm, bm), columns], top, total)
    one_top = jnp.max(top, axis=0, keepdims=True)
    one_total = jnp.sum(total * jnp.exp(top - one_top), axis=0, keepdims=True)
    msg_ref[...] = msg_in[...]
    slots = pair_slots(chips)[2 * k : 2 * k + 2]
    for j, (owner, swap) in enumerate(slots):
        lanes = slice(j * LANES, (j + 1) * LANES)
        msg_ref[pl.ds(owner, 1), :] = swapped(one_top[:, lanes], swap)
        msg_ref[pl.ds(chips + owner, 1), :] = swapped(one_total[:, lanes], swap)
    if accum_copy is not None:
        accum_copy.wait()


def score(k, chips, blocks, accum, held, state):
    rows, feats = state[1].shape
    bm = min(512, rows)
    width = 2 * LANES
    base = len(blocks) + 2
    place = in_hbm if k == 0 else in_vmem
    inputs = [place(b) for b in blocks] + [in_hbm(accum)] + [in_vmem(s) for s in state]
    specs = [ANY if k == 0 else VM] * len(blocks) + [ANY]
    aliases = {base + i: 1 + i for i in range(4)}
    specs += [VM] * (len(inputs) - len(specs))
    cfg = (chips, k, held, bm, len(blocks))
    return pl.pallas_call(
        functools.partial(score_kernel, cfg),
        name=f"score_{k}",
        out_shape=[pltpu.VMEM(a.shape, a.dtype) for a in state],
        in_specs=specs,
        out_specs=[VM] * 5,
        input_output_aliases=aliases,
        scratch_shapes=[pltpu.SemaphoreType.DMA, pltpu.SemaphoreType.DMA],
        compiler_params=pltpu.CompilerParams(vmem_limit_bytes=SCOPED),
        cost_estimate=pl.CostEstimate(
            flops=2 * rows * feats * width,
            bytes_accessed=(rows + width) * feats * 2,
            transcendentals=rows * width,
        ),
    )(*inputs)


def small_call(kernel, name, shape, inputs, pinned):
    n = len(inputs)

    def with_pinned(*refs):
        kernel(*refs[:n], refs[n + len(pinned)])

    out, *pinned = pl.pallas_call(
        with_pinned,
        name=name,
        out_shape=[pltpu.VMEM(shape, inputs[0].dtype)]
        + [pltpu.VMEM(p.shape, p.dtype) for p in pinned],
        in_specs=[VM] * (n + len(pinned)),
        out_specs=[VM] * (1 + len(pinned)),
        input_output_aliases={n + i: 1 + i for i in range(len(pinned))},
        compiler_params=pltpu.CompilerParams(vmem_limit_bytes=SCOPED),
    )(*[in_vmem(a) for a in [*inputs, *pinned]])
    return out, pinned


def head_kernel(x_ref, out_ref):
    out_ref[...] = x_ref[: out_ref.shape[0], :]


def merge_kernel(*refs):
    top, total, labels = merge_parts([r[...] for r in refs[:-1]])
    n = top.shape[0]
    refs[-1][:n] = top
    refs[-1][n : 2 * n] = total
    refs[-1][2 * n :] = labels


def update_kernel(cfg, *refs):
    chips, n_msgs, bm, held_blocks, bn = cfg
    msgs, refs = refs[:n_msgs], refs[n_msgs:]
    other_ref, accum_hbm, logits_ref, x_ref = refs[:4]
    w_ref, acc_ref, out_w, out_acc, out_lse = refs[6:11]
    canon_s, lse_s, label_s, delta_s, read_sem, acc_sem, w_sem = refs[11:]
    rows, batch = logits_ref.shape
    feats = x_ref.shape[1]
    blocks = rows // bm

    chip, core, _ = whereabouts(chips)
    rank = lax.axis_index("blk") * lax.axis_size("cls") + lax.axis_index("cls")
    first_class = rank * rows
    top, total, labels = merge_parts([m[...] for m in msgs])
    slab_lse = top + jnp.log(total)
    other = other_ref[...]
    high = jnp.maximum(slab_lse, other)
    lse = high + jnp.log(jnp.exp(slab_lse - high) + jnp.exp(other - high))
    canon_s[:chips] = lse
    canon_s[chips:] = labels
    own = canon_s[pl.ds(chip, 1), :]
    out_lse[...] = jnp.where(core == 0, own[:, : LANES // 2], own[:, LANES // 2 :])
    for j, (owner, swap) in enumerate(pair_slots(chips)):
        lanes = pl.ds(j * LANES, LANES)
        lse_s[:, lanes] = swapped(canon_s[pl.ds(owner, 1), :], swap)
        label_s[:, lanes] = (
            swapped(canon_s[pl.ds(chips + owner, 1), :], swap).astype(i32) - first_class
        )

    def make_delta(i, to):
        r0 = pl.multiple_of(i * bm, bm)
        chance = jnp.exp(logits_ref[pl.ds(r0, bm), :] - lse_s[...])
        row = lax.broadcasted_iota(i32, (bm, batch), 0)
        hit = row == (label_s[...] - r0)
        delta_s[to] = jnp.where(hit, chance - 1.0, chance).astype(bf16)

    def rows_of(i):
        return pl.ds(pl.multiple_of(i * bm, bm), bm)

    def read(i):
        slot = lax.rem(i, held_blocks)
        return pltpu.make_async_copy(
            accum_hbm.at[rows_of(i)], acc_ref.at[rows_of(slot)], read_sem.at[slot]
        )

    def writes(i):
        slot = lax.rem(i, held_blocks)
        return (
            pltpu.make_async_copy(
                acc_ref.at[rows_of(slot)], out_acc.at[rows_of(i)], acc_sem.at[slot]
            ),
            pltpu.make_async_copy(
                w_ref.at[rows_of(i)], out_w.at[rows_of(i)], w_sem.at[lax.rem(i, LAG + 1)]
            ),
        )

    make_delta(0, 0)

    def step(i, carry):
        now = lax.rem(i, 2)
        slot = lax.rem(i, held_blocks)

        @pl.when(i >= held_blocks)
        def _():
            read(i).wait()

        make_delta(jnp.minimum(i + 1, blocks - 1), 1 - now)
        for n in range(feats // bn):
            cols = pl.ds(n * bn, bn)
            grad = jnp.dot(delta_s[now], x_ref[:, cols], preferred_element_type=f32)
            new_acc = acc_ref[rows_of(slot), cols] + grad * grad
            acc_ref[rows_of(slot), cols] = new_acc
            old = w_ref[rows_of(i), cols].astype(f32)
            w_ref[rows_of(i), cols] = (
                old - 0.05 * grad / (jnp.sqrt(new_acc) + 1e-10)
            ).astype(bf16)

        @pl.when(i >= LAG)
        def _():
            for copy in writes(i - LAG):
                copy.wait()

            @pl.when(i - LAG + held_blocks < blocks)
            def _():
                read(i - LAG + held_blocks).start()

        for copy in writes(i):
            copy.start()
        return carry

    lax.fori_loop(0, blocks, step, 0)
    for i in range(max(0, blocks - LAG), blocks):
        for copy in writes(i):
            copy.wait()


def update(chips, msgs, other, accum, logits, x, weight_v, acc_v, bm):
    rows, batch = logits.shape
    feats = x.shape[1]
    held_blocks = acc_v.shape[0] // bm
    bn = min(512, feats)
    inputs = [in_vmem(m) for m in msgs] + [other, in_hbm(accum)] + [
        in_vmem(a) for a in (logits, x, weight_v, acc_v)
    ]
    n = len(msgs)
    cfg = (chips, n, bm, held_blocks, bn)
    outs = pl.pallas_call(
        functools.partial(update_kernel, cfg),
        name="update",
        out_shape=[
            pltpu.VMEM(weight_v.shape, bf16),
            pltpu.VMEM(acc_v.shape, f32),
            pltpu.HBM((rows, feats), bf16),
            pltpu.HBM((rows, feats), f32),
            jax.ShapeDtypeStruct((1, LANES // 2), f32),
        ],
        in_specs=[VM] * n + [VM, ANY, VM, VM, VM, VM],
        out_specs=[VM, VM, ANY, ANY, VM],
        input_output_aliases={n + 4: 0, n + 5: 1},
        scratch_shapes=[
            pltpu.VMEM((2 * chips, LANES), f32),
            pltpu.VMEM((1, batch), f32),
            pltpu.VMEM((1, batch), i32),
            pltpu.VMEM((2, bm, batch), bf16),
            pltpu.SemaphoreType.DMA((held_blocks,)),
            pltpu.SemaphoreType.DMA((held_blocks,)),
            pltpu.SemaphoreType.DMA((LAG + 1,)),
        ],
        compiler_params=pltpu.CompilerParams(vmem_limit_bytes=SCOPED),
        cost_estimate=pl.CostEstimate(
            flops=2 * rows * feats * batch,
            bytes_accessed=rows * feats * 10,
            transcendentals=rows * batch,
        ),
    )(*inputs)
    return outs[2:]


def exchange_stats(message, pinned, blk_size, cls_size):
    bits_cls = cls_size.bit_length() - 1
    bits = bits_cls + blk_size.bit_length() - 1
    core, y = bits_cls, bits_cls + 1
    rest = [b for b in range(bits) if b not in (core, y, 0)]
    groups = [(core,), (0, y)] + [tuple(rest[i : i + 2]) for i in range(0, len(rest), 2)]
    messages = [message]
    for group in groups:
        if len(messages) > 1:
            message, pinned = small_call(
                merge_kernel, "merge_stats", message.shape, messages, pinned
            )
        messages = [message]
        for pick in range(1, 2 ** len(group)):
            flip = sum(1 << b for at, b in enumerate(group) if pick >> at & 1)
            pairs = [(d, d ^ flip) for d in range(blk_size * cls_size)]
            messages.append(lax.ppermute(message, ("blk", "cls"), pairs))
    return messages, pinned


def body(features, labels, offset, other_lse, weight, accum):
    blk_size, cls_size = lax.axis_size("blk"), lax.axis_size("cls")
    chips = blk_size // 2
    steps = chips // 2
    block, feats = features.shape
    rows = weight.shape[0]
    batch = block * blk_size
    bm = min(256 * 1024 // batch, rows)
    held_rows = min(rows, HELD_BYTES // (feats * 4))

    def swap_cores(x):
        return lax.ppermute(x, "blk", [(d, d ^ 1) for d in range(blk_size)])

    def round_ring(x):
        return lax.ppermute(x, "blk", ring_pairs(chips))

    sibling = swap_cores(features)
    pair = jnp.concatenate([features, sibling], axis=0)
    came = round_ring(pair)
    *pinned, message = hold(weight, pair, labels, offset, chips, batch, held_rows)
    state = [message, *pinned]
    came, state[0] = lax.optimization_barrier((came, state[0]))
    blocks = [came]
    for k in range(steps):
        if k < steps - 1:
            crossed = swap_cores(came)
            if k == steps - 2:
                came, state[1:] = small_call(head_kernel, "head", (block, feats), [came], state[1:])
            came = round_ring(came)
        cut = [min(held_rows, held_rows * i // 2) for i in (k, k + 1)] if k < 2 else [0, 0]
        state = list(score(k, chips, blocks, accum, tuple(cut), state))
        if k < steps - 1:
            came, state[0] = lax.optimization_barrier((came, state[0]))
            blocks = [crossed, came] + ([swap_cores(came)] if k == steps - 2 else [])
    messages, pinned = exchange_stats(state[0], state[1:], blk_size, cls_size)
    weight_v, logits, x, acc_v = pinned
    new_weight, new_accum, lse = update(
        chips, messages, other_lse.reshape(chips, LANES), accum, logits, x, weight_v, acc_v, bm
    )
    return (new_weight, new_accum, lse.reshape(block))


def solution(mesh):
    in_specs = (
        P("blk", None),
        P("blk"),
        P(),
        P(),
        P(("blk", "cls"), None),
        P(("blk", "cls"), None),
    )
    out_specs = (P(("blk", "cls"), None), P(("blk", "cls"), None), P("blk"))
    return jax.shard_map(body, mesh=mesh, in_specs=in_specs, out_specs=out_specs, check_vma=False)
```

time: 232 us -> 102 us (0.44)
  blocking collectives: 93.2 us -> 0 us
  matrix products: 73.5 us -> 0 us
  Pallas kernels: 0 us -> 72.2 us
  waiting for transfers between devices: 39 us -> 9.05 us
  starting transfers between devices: 0.04 us -> 17.9 us
  between operations: 15.3 us -> 1.56 us
  other arithmetic: 8.11 us -> 0 us
    dot_general x2 -> x0, matrix products: 73.5 us -> none  [the longest x1 49.7 us: gradient_term(): lax.dot_general(delta, rows, (((0,), (0,)), ((), ())), preferred_element_...]
    pallas_call x0 -> x9, Pallas kernels: none -> 72.2 us  [the longest x1 39.1 us: update(): pl.pallas_call(functools.partial(update_kernel, cfg), name='update', out_...]
    psum x1 -> x0, blocking collectives: 40.2 us -> none  [body(): lax.psum(jnp.sum(jnp.exp(logits - top[:, None]), axis=1), ('blk', 'cls'))]
    pmax x1 -> x0, blocking collectives: 39.2 us -> none  [body(): top = lax.pmax(local_top, ('blk', 'cls'))]
    all_gather x1 -> x0, waiting for transfers between devices: 38.3 us -> none  [body(): lax.all_gather(features, 'blk', axis=0, tiled=True)]
    ppermute x0 -> x16, starting transfers between devices: none -> 17.9 us  [the longest x4 8.52 us: round_ring(): return lax.ppermute(x, 'blk', ring_pairs(chips))]
    unnamed x1 -> x0, blocking collectives: 13.8 us -> none
    ppermute x0 -> x16, waiting for transfers between devices: none -> 9.05 us  [the longest x7 6.75 us: exchange_stats(): messages.append(lax.ppermute(message, ('blk', 'cls'), pairs))]
  transfers between devices with their start and end apart: 1 -> 16, of which waited for: 1 -> 9; matrix products, arithmetic and copies ran while one was open for 1% -> 1% of each run, Pallas kernels for 0% -> 28%
where the time goes in v1:
time: 102 us
  Pallas kernels  72.2 us (71%)
  starting transfers between devices  17.9 us (18%)
  waiting for transfers between devices  9.05 us (9%)
  between operations  1.56 us (2%)
    pallas_call x1, Pallas kernels, update(): pl.pallas_call(functools.partial(update_kernel, cfg), name='update', out_...  39.1 us
    pallas_call x4, Pallas kernels, score(): pl.pallas_call(functools.partial(score_kernel, cfg), name=f'score_{k}', o...  27 us
    ppermute x4, starting transfers between devices, round_ring(): return lax.ppermute(x, 'blk', ring_pairs(chips))  8.52 us
    ppermute x7, starting transfers between devices, exchange_stats(): messages.append(lax.ppermute(message, ('blk', 'cls'), pairs))  8.21 us
    ppermute x7, waiting for transfers between devices, exchange_stats(): messages.append(lax.ppermute(message, ('blk', 'cls'), pairs))  6.75 us
    pallas_call x1, Pallas kernels, hold(): pl.pallas_call(functools.partial(hold_kernel, chips, pieces), name='hold_...  6.08 us
  transfers between devices with their start and end apart: 16, of which 9 were waited for; matrix products, arithmetic and copies ran while one was open for 1% of the time, Pallas kernels for 28%

profile of v1, /device:TPU:0, one launch (start us, length us, event | category | flops | bytes accessed | tf_op | source)
XLA Modules:
  0.0 101.7 jit_solution(3182245758889659920)
XLA Ops:
  0.6 0.5 collective-permute-start
  1.1 1.0 constant_dynamic-update-slice_fusion.1
  2.1 0.4 collective-permute-done
  2.5 0.0 copy-start
  2.6 3.0 %collective-permute-start.1 = (bf16[128,2048]{1,0:T(8,128)(2,1)S(1)}, bf16[128,2048]{1,0:T(8,128)(2,1)S(1)}, u32[]{:S(2)}, u32[]{:S(2)}) collective-permute-start(bf16[128,2048]{1,0:T(8,128)(2,1)S(1)} %constant_dynamic-update-slice_fusion.pair_hbm), channel_id=1, source_target_pairs={{0,8},{2,6},{8,16},{10,2},{16,24},{18,10},{24,28},{26,18},{28,20},... | collective-permute-start | bytes 1572872 | tf_op jit(solution)/shard_map/ppermute | solution.py:429
  6.2 0.0 copy-done
  6.2 6.1 %hold_weight.1 = (bf16[4096,2048]{1,0:T(8,128)(2,1)S(1)}, f32[4096,1024]{1,0:T(8,128)S(1)}, bf16[1024,2048]{1,0:T(8,128)(2,1)S(1)}, f32[2048,2048]{1,0:T(8,128)S(1)}, f32[24,128]{1,0:T(8,128)S(1)}) custom-call(bf16[4096,2048]{1,0:T(8,128)(2,1)} %w_hbm.1, bf16[128,2048]{1,0:T(8,128)(2,1)} %copy-done, s32[1,64]{1,0:T(1,128)} %bitcast.4, s32[1]{0:T(128)S(6)} %copy.70.offset_ref), custom_call_target="tpu_custom_call" | custom-call | bytes 16777216 | tf_op jit(solution)/shard_map/hold_weight/pallas_call | solution.py:117
  12.3 0.4 collective-permute-done.1.refs_0_
  12.7 0.0 copy-start.1
  12.7 2.1 %collective-permute-start.2 = (bf16[128,2048]{1,0:T(8,128)(2,1)S(1)}, bf16[128,2048]{1,0:T(8,128)(2,1)S(1)}, u32[]{:S(2)}, u32[]{:S(2)}) collective-permute-start(bf16[128,2048]{1,0:T(8,128)(2,1)S(1)} %collective-permute-done.1.refs_0_), channel_id=1, source_target_pairs={{0,8},{2,6},{8,16},{10,2},{16,24},{18,10},{24,28},{26,18},{28,20},... | collective-permute-start | bytes 1572872 | tf_op jit(solution)/shard_map/ppermute | solution.py:429
  14.7 0.0 collective-permute-start.4
  14.7 0.0 copy-done.1
  14.7 8.5 %score_0.1 = (f32[24,128]{1,0:T(8,128)S(1)}, bf16[4096,2048]{1,0:T(8,128)(2,1)S(1)}, f32[4096,1024]{1,0:T(8,128)S(1)}, bf16[1024,2048]{1,0:T(8,128)(2,1)S(1)}, f32[2048,2048]{1,0:T(8,128)S(1)}) custom-call(bf16[128,2048]{1,0:T(8,128)(2,1)} %copy-done.1, ...), custom_call_target="tpu_custom_call", output_to_operand_aliasing={{1}: (3, {}), {2}: (4, {}), {3}: (5, {}), {4}: (6, {})} | custom-call | flops 4294967296 | bytes 17825792 | tf_op jit(solution)/shard_map/score_0/pallas_call | solution.py:209
  23.3 0.0 collective-permute-done.2.refs_1_
  23.3 1.6 %collective-permute-start.3 = (bf16[128,2048]{1,0:T(8,128)(2,1)S(1)}, bf16[128,2048]{1,0:T(8,128)(2,1)S(1)}, u32[]{:S(2)}, u32[]{:S(2)}) collective-permute-start(bf16[128,2048]{1,0:T(8,128)(2,1)S(1)} %collective-permute-done.2.refs_1_), channel_id=1, source_target_pairs={{0,8},{2,6},{8,16},{10,2},{16,24},{18,10},{24,28},{26,18},{28,20},... | collective-permute-start | bytes 1572872 | tf_op jit(solution)/shard_map/ppermute | solution.py:429
  24.9 0.0 collective-permute-start.7
  24.9 0.0 collective-permute-done.4.refs_0_
  24.9 8.3 %score_1.1 = (f32[24,128]{1,0:T(8,128)S(1)}, bf16[4096,2048]{1,0:T(8,128)(2,1)S(1)}, f32[4096,1024]{1,0:T(8,128)S(1)}, bf16[1024,2048]{1,0:T(8,128)(2,1)S(1)}, f32[2048,2048]{1,0:T(8,128)S(1)}) custom-call(bf16[128,2048]{1,0:T(8,128)(2,1)S(1)} %collective-permute-done.4.refs_0_, ...), custom_call_target="tpu_custom_call", output_to_operand_aliasing={{1}: (4, {}), {2}: (5, {}), {3}: (6, {}), {4}: (7, {})} | custom-call | flops 4294967296 | bytes 17825792 | tf_op jit(solution)/shard_map/score_1/pallas_call | solution.py:209
  33.2 0.0 collective-permute-done.3.refs_0_.refs_1_
  33.2 0.6 collective-permute-start.5
  33.8 1.8 %collective-permute-start.6 = (bf16[64,2048]{1,0:T(8,128)(2,1)S(1)}, bf16[64,2048]{1,0:T(8,128)(2,1)S(1)}, u32[]{:S(2)}, u32[]{:S(2)}) collective-permute-start(bf16[64,2048]{1,0:T(8,128)(2,1)S(1)} %get-tuple-element.74), channel_id=1, source_target_pairs={{0,8},{2,6},{8,16},{10,2},{16,24},{18,10},{24,28},{26,18},{28,20},... | collective-permute-start | bytes 786440 | tf_op jit(solution)/shard_map/ppermute | solution.py:429
  35.6 0.0 collective-permute-done.7.refs_0_
  35.6 5.1 %score_2.1 = (f32[24,128]{1,0:T(8,128)S(1)}, bf16[4096,2048]{1,0:T(8,128)(2,1)S(1)}, f32[4096,1024]{1,0:T(8,128)S(1)}, bf16[1024,2048]{1,0:T(8,128)(2,1)S(1)}, f32[2048,2048]{1,0:T(8,128)S(1)}) custom-call(bf16[128,2048]{1,0:T(8,128)(2,1)S(1)} %collective-permute-done.7.refs_0_, ...), custom_call_target="tpu_custom_call", output_to_operand_aliasing={{1}: (4, {}), {2}: (5, {}), {3}: (6, {}), {4}: (7, {})} | custom-call | flops 4294967296 | bytes 17825792 | tf_op jit(solution)/shard_map/score_2/pallas_call | solution.py:209
  40.8 0.0 collective-permute-done.6.refs_1_
  40.8 0.1 collective-permute-start.8
  40.9 1.5 %collective-permute-done.8.refs_2_ = bf16[64,2048]{1,0:T(8,128)(2,1)S(1)} collective-permute-done((bf16[64,2048]{1,0:T(8,128)(2,1)S(1)}, bf16[64,2048]{1,0:T(8,128)(2,1)S(1)}, u32[]{:S(2)}, u32[]{:S(2)}) %collective-permute-start.8) | collective-permute-done | bytes 262176 | tf_op jit(solution)/shard_map/ppermute | solution.py:426
  42.4 0.0 collective-permute-done.5.refs_0_
  42.4 5.1 %score_3.1 = (f32[24,128]{1,0:T(8,128)S(1)}, bf16[4096,2048]{1,0:T(8,128)(2,1)S(1)}, f32[4096,1024]{1,0:T(8,128)S(1)}, bf16[1024,2048]{1,0:T(8,128)(2,1)S(1)}, f32[2048,2048]{1,0:T(8,128)S(1)}) custom-call(bf16[128,2048]{1,0:T(8,128)(2,1)S(1)} %collective-permute-done.5.refs_0_, ...), custom_call_target="tpu_custom_call", output_to_operand_aliasing={{1}: (5, {}), {2}: (6, {}), {3}: (7, {}), {4}: (8, {})} | custom-call | flops 4294967296 | bytes 17825792 | tf_op jit(solution)/shard_map/score_3/pallas_call | solution.py:209
  47.5 0.2 collective-permute-start.9
  47.7 1.0 %collective-permute-done.9.refs_1_ = f32[24,128]{1,0:T(8,128)S(1)} collective-permute-done((f32[24,128]{1,0:T(8,128)S(1)}, f32[24,128]{1,0:T(8,128)S(1)}, u32[]{:S(2)}, u32[]{:S(2)}) %collective-permute-start.9) | collective-permute-done | bytes 12320 | tf_op jit(solution)/shard_map/ppermute | solution.py:411
  48.7 1.4 %collective-permute-start.12 = (f32[24,128]{1,0:T(8,128)S(1)}, f32[24,128]{1,0:T(8,128)S(1)}, u32[]{:S(2)}, u32[]{:S(2)}) collective-permute-start(f32[24,128]{1,0:T(8,128)S(1)} %get-tuple-element.92.refs_0_), channel_id=1, source_target_pairs={{0,5},{1,4},{2,7},{3,6},{4,1},{5,0},{6,3},{7,2},{8,13},{9,12},{10,... | collective-permute-start | bytes 36872 | tf_op jit(solution)/shard_map/ppermute | solution.py:411
  50.2 1.6 %collective-permute-start.11 = (f32[24,128]{1,0:T(8,128)S(1)}, f32[24,128]{1,0:T(8,128)S(1)}, u32[]{:S(2)}, u32[]{:S(2)}) collective-permute-start(f32[24,128]{1,0:T(8,128)S(1)} %get-tuple-element.92.refs_0_), channel_id=1, source_target_pairs={{0,4},{1,5},{2,6},{3,7},{4,0},{5,1},{6,2},{7,3},{8,12},{9,13},{10,... | collective-permute-start | bytes 36872 | tf_op jit(solution)/shard_map/ppermute | solution.py:411
  51.7 0.5 collective-permute-start.10
  52.3 1.1 %collective-permute-done.12.refs_3_ = f32[24,128]{1,0:T(8,128)S(1)} collective-permute-done((f32[24,128]{1,0:T(8,128)S(1)}, f32[24,128]{1,0:T(8,128)S(1)}, u32[]{:S(2)}, u32[]{:S(2)}) %collective-permute-start.12) | collective-permute-done | bytes 12320 | tf_op jit(solution)/shard_map/ppermute | solution.py:411
  53.4 0.5 collective-permute-done.11.refs_2_
  53.9 1.6 %collective-permute-done.10.refs_1_ = f32[24,128]{1,0:T(8,128)S(1)} collective-permute-done((f32[24,128]{1,0:T(8,128)S(1)}, f32[24,128]{1,0:T(8,128)S(1)}, u32[]{:S(2)}, u32[]{:S(2)}) %collective-permute-start.10) | collective-permute-done | bytes 12320 | tf_op jit(solution)/shard_map/ppermute | solution.py:411
  55.5 2.4 %collective-permute-start.15 = (f32[24,128]{1,0:T(8,128)S(1)}, f32[24,128]{1,0:T(8,128)S(1)}, u32[]{:S(2)}, u32[]{:S(2)}) collective-permute-start(f32[24,128]{1,0:T(8,128)S(1)} %get-tuple-element.97.refs_0_), channel_id=1, source_target_pairs={{0,24},{1,25},{2,26},{3,27},{4,28},{5,29},{6,30},{7,31},{8,16},{9,... | collective-permute-start | bytes 36872 | tf_op jit(solution)/shard_map/ppermute | solution.py:411
  57.9 0.6 collective-permute-start.14
  58.5 1.4 %collective-permute-start.13 = (f32[24,128]{1,0:T(8,128)S(1)}, f32[24,128]{1,0:T(8,128)S(1)}, u32[]{:S(2)}, u32[]{:S(2)}) collective-permute-start(f32[24,128]{1,0:T(8,128)S(1)} %get-tuple-element.97.refs_0_), channel_id=1, source_target_pairs={{0,8},{1,9},{2,10},{3,11},{4,12},{5,13},{6,14},{7,15},{8,0},{9,1},... | collective-permute-start | bytes 36872 | tf_op jit(solution)/shard_map/ppermute | solution.py:411
  59.9 1.1 %collective-permute-done.15.refs_3_ = f32[24,128]{1,0:T(8,128)S(1)} collective-permute-done((f32[24,128]{1,0:T(8,128)S(1)}, f32[24,128]{1,0:T(8,128)S(1)}, u32[]{:S(2)}, u32[]{:S(2)}) %collective-permute-start.15) | collective-permute-done | bytes 12320 | tf_op jit(solution)/shard_map/ppermute | solution.py:411
  61.0 1.5 %collective-permute-done.14.refs_2_ = f32[24,128]{1,0:T(8,128)S(1)} collective-permute-done((f32[24,128]{1,0:T(8,128)S(1)}, f32[24,128]{1,0:T(8,128)S(1)}, u32[]{:S(2)}, u32[]{:S(2)}) %collective-permute-start.14) | collective-permute-done | bytes 12320 | tf_op jit(solution)/shard_map/ppermute | solution.py:411
  62.5 0.0 collective-permute-done.13.refs_1_
  62.5 39.1 %update.1 = (bf16[4096,2048]{1,0:T(8,128)(2,1)S(1)}, f32[2048,2048]{1,0:T(8,128)S(1)}, bf16[4096,2048]{1,0:T(8,128)(2,1)}, f32[4096,2048]{1,0:T(8,128)}, f32[1,64]{1,0:T(1,128)}) custom-call(f32[24,128]{1,0:T(8,128)S(1)} %get-tuple-element.97.refs_0_, f32[24,128]{1,0:T(8,128)S(1)} %collective-permute-done.13.refs_1_, ...), custom_call_target="tpu_custom_call", output_to_operand_aliasing={{0}: (8, {}), {1}: (9, {})} | custom-call | flops 17179869184 | bytes 83886080 | tf_op jit(solution)/shard_map/update/pallas_call | solution.py:363
  (4 shorter events, 0.1 us)
Async XLA Ops:
  0.6 1.9 %collective-permute-start = (bf16[64,2048]{1,0:T(8,128)(2,1)}, bf16[64,2048]{1,0:T(8,128)(2,1)S(1)}, u32[]{:S(2)}, u32[]{:S(2)}) collective-permute-start(bf16[64,2048]{1,0:T(8,128)(2,1)} %param.6), channel_id=1, source_target_pairs={{0,2},{2,0},{4,6},{6,4},{8,10},{10,8},{12,14},{14,12},{16,18},{18,... | collective-permute-start | bytes 786440 | tf_op jit(solution)/shard_map/ppermute | solution.py:426
  2.5 3.7 %copy-start = (bf16[128,2048]{1,0:T(8,128)(2,1)}, bf16[128,2048]{1,0:T(8,128)(2,1)S(1)}, u32[]{:S(2)}) copy-start(bf16[128,2048]{1,0:T(8,128)(2,1)S(1)} %constant_dynamic-update-slice_fusion.pair_hbm) | copy-start | bytes 1572868
  2.6 10.1 %collective-permute-start.1 = (bf16[128,2048]{1,0:T(8,128)(2,1)S(1)}, bf16[128,2048]{1,0:T(8,128)(2,1)S(1)}, u32[]{:S(2)}, u32[]{:S(2)}) collective-permute-start(bf16[128,2048]{1,0:T(8,128)(2,1)S(1)} %constant_dynamic-update-slice_fusion.pair_hbm), channel_id=1, source_target_pairs={{0,8},{2,6},{8,16},{10,2},{16,24},{18,10},{24,28},{26,18},{28,20},... | collective-permute-start | bytes 1572872 | tf_op jit(solution)/shard_map/ppermute | solution.py:429
  12.7 2.1 %copy-start.1 = (bf16[128,2048]{1,0:T(8,128)(2,1)}, bf16[128,2048]{1,0:T(8,128)(2,1)S(1)}, u32[]{:S(2)}) copy-start(bf16[128,2048]{1,0:T(8,128)(2,1)S(1)} %collective-permute-done.1.refs_0_) | copy-start | bytes 1572868
  12.7 10.6 %collective-permute-start.2 = (bf16[128,2048]{1,0:T(8,128)(2,1)S(1)}, bf16[128,2048]{1,0:T(8,128)(2,1)S(1)}, u32[]{:S(2)}, u32[]{:S(2)}) collective-permute-start(bf16[128,2048]{1,0:T(8,128)(2,1)S(1)} %collective-permute-done.1.refs_0_), channel_id=1, source_target_pairs={{0,8},{2,6},{8,16},{10,2},{16,24},{18,10},{24,28},{26,18},{28,20},... | collective-permute-start | bytes 1572872 | tf_op jit(solution)/shard_map/ppermute | solution.py:429
  14.7 10.2 %collective-permute-start.4 = (bf16[128,2048]{1,0:T(8,128)(2,1)S(1)}, bf16[128,2048]{1,0:T(8,128)(2,1)S(1)}, u32[]{:S(2)}, u32[]{:S(2)}) collective-permute-start(bf16[128,2048]{1,0:T(8,128)(2,1)S(1)} %collective-permute-done.1.refs_0_), channel_id=1, source_target_pairs={{0,2},{2,0},{4,6},{6,4},{8,10},{10,8},{12,14},{14,12},{16,18},{18,... | collective-permute-start | bytes 1572872 | tf_op jit(solution)/shard_map/ppermute | solution.py:426
  23.3 9.9 %collective-permute-start.3 = (bf16[128,2048]{1,0:T(8,128)(2,1)S(1)}, bf16[128,2048]{1,0:T(8,128)(2,1)S(1)}, u32[]{:S(2)}, u32[]{:S(2)}) collective-permute-start(bf16[128,2048]{1,0:T(8,128)(2,1)S(1)} %collective-permute-done.2.refs_1_), channel_id=1, source_target_pairs={{0,8},{2,6},{8,16},{10,2},{16,24},{18,10},{24,28},{26,18},{28,20},... | collective-permute-start | bytes 1572872 | tf_op jit(solution)/shard_map/ppermute | solution.py:429
  24.9 10.7 %collective-permute-start.7 = (bf16[128,2048]{1,0:T(8,128)(2,1)S(1)}, bf16[128,2048]{1,0:T(8,128)(2,1)S(1)}, u32[]{:S(2)}, u32[]{:S(2)}) collective-permute-start(bf16[128,2048]{1,0:T(8,128)(2,1)S(1)} %collective-permute-done.2.refs_1_), channel_id=1, source_target_pairs={{0,2},{2,0},{4,6},{6,4},{8,10},{10,8},{12,14},{14,12},{16,18},{18,... | collective-permute-start | bytes 1572872 | tf_op jit(solution)/shard_map/ppermute | solution.py:426
  33.2 9.1 %collective-permute-start.5 = (bf16[128,2048]{1,0:T(8,128)(2,1)S(1)}, bf16[128,2048]{1,0:T(8,128)(2,1)S(1)}, u32[]{:S(2)}, u32[]{:S(2)}) collective-permute-start(bf16[128,2048]{1,0:T(8,128)(2,1)S(1)} %collective-permute-done.3.refs_0_.refs_1_), channel_id=1, source_target_pairs={{0,2},{2,0},{4,6},{6,4},{8,10},{10,8},{12,14},{14,12},{16,18},{18,... | collective-permute-start | bytes 1572872 | tf_op jit(solution)/shard_map/ppermute | solution.py:426
  33.8 6.9 %collective-permute-start.6 = (bf16[64,2048]{1,0:T(8,128)(2,1)S(1)}, bf16[64,2048]{1,0:T(8,128)(2,1)S(1)}, u32[]{:S(2)}, u32[]{:S(2)}) collective-permute-start(bf16[64,2048]{1,0:T(8,128)(2,1)S(1)} %get-tuple-element.74), channel_id=1, source_target_pairs={{0,8},{2,6},{8,16},{10,2},{16,24},{18,10},{24,28},{26,18},{28,20},... | collective-permute-start | bytes 786440 | tf_op jit(solution)/shard_map/ppermute | solution.py:429
  40.8 1.6 %collective-permute-start.8 = (bf16[64,2048]{1,0:T(8,128)(2,1)S(1)}, bf16[64,2048]{1,0:T(8,128)(2,1)S(1)}, u32[]{:S(2)}, u32[]{:S(2)}) collective-permute-start(bf16[64,2048]{1,0:T(8,128)(2,1)S(1)} %collective-permute-done.6.refs_1_), channel_id=1, source_target_pairs={{0,2},{2,0},{4,6},{6,4},{8,10},{10,8},{12,14},{14,12},{16,18},{18,... | collective-permute-start | bytes 786440 | tf_op jit(solution)/shard_map/ppermute | solution.py:426
  47.5 1.2 %collective-permute-start.9 = (f32[24,128]{1,0:T(8,128)S(1)}, f32[24,128]{1,0:T(8,128)S(1)}, u32[]{:S(2)}, u32[]{:S(2)}) collective-permute-start(f32[24,128]{1,0:T(8,128)S(1)} %get-tuple-element.87.refs_0_), channel_id=1, source_target_pairs={{0,2},{1,3},{2,0},{3,1},{4,6},{5,7},{6,4},{7,5},{8,10},{9,11},{10,... | collective-permute-start | bytes 36872 | tf_op jit(solution)/shard_map/ppermute | solution.py:411
  48.7 4.7 %collective-permute-start.12 = (f32[24,128]{1,0:T(8,128)S(1)}, f32[24,128]{1,0:T(8,128)S(1)}, u32[]{:S(2)}, u32[]{:S(2)}) collective-permute-start(f32[24,128]{1,0:T(8,128)S(1)} %get-tuple-element.92.refs_0_), channel_id=1, source_target_pairs={{0,5},{1,4},{2,7},{3,6},{4,1},{5,0},{6,3},{7,2},{8,13},{9,12},{10,... | collective-permute-start | bytes 36872 | tf_op jit(solution)/shard_map/ppermute | solution.py:411
  50.2 3.7 %collective-permute-start.11 = (f32[24,128]{1,0:T(8,128)S(1)}, f32[24,128]{1,0:T(8,128)S(1)}, u32[]{:S(2)}, u32[]{:S(2)}) collective-permute-start(f32[24,128]{1,0:T(8,128)S(1)} %get-tuple-element.92.refs_0_), channel_id=1, source_target_pairs={{0,4},{1,5},{2,6},{3,7},{4,0},{5,1},{6,2},{7,3},{8,12},{9,13},{10,... | collective-permute-start | bytes 36872 | tf_op jit(solution)/shard_map/ppermute | solution.py:411
  51.7 3.7 %collective-permute-start.10 = (f32[24,128]{1,0:T(8,128)S(1)}, f32[24,128]{1,0:T(8,128)S(1)}, u32[]{:S(2)}, u32[]{:S(2)}) collective-permute-start(f32[24,128]{1,0:T(8,128)S(1)} %get-tuple-element.92.refs_0_), channel_id=1, source_target_pairs={{0,1},{1,0},{2,3},{3,2},{4,5},{5,4},{6,7},{7,6},{8,9},{9,8},{10,11... | collective-permute-start | bytes 36872 | tf_op jit(solution)/shard_map/ppermute | solution.py:411
  55.5 5.6 %collective-permute-start.15 = (f32[24,128]{1,0:T(8,128)S(1)}, f32[24,128]{1,0:T(8,128)S(1)}, u32[]{:S(2)}, u32[]{:S(2)}) collective-permute-start(f32[24,128]{1,0:T(8,128)S(1)} %get-tuple-element.97.refs_0_), channel_id=1, source_target_pairs={{0,24},{1,25},{2,26},{3,27},{4,28},{5,29},{6,30},{7,31},{8,16},{9,... | collective-permute-start | bytes 36872 | tf_op jit(solution)/shard_map/ppermute | solution.py:411
  57.9 4.6 %collective-permute-start.14 = (f32[24,128]{1,0:T(8,128)S(1)}, f32[24,128]{1,0:T(8,128)S(1)}, u32[]{:S(2)}, u32[]{:S(2)}) collective-permute-start(f32[24,128]{1,0:T(8,128)S(1)} %get-tuple-element.97.refs_0_), channel_id=1, source_target_pairs={{0,16},{1,17},{2,18},{3,19},{4,20},{5,21},{6,22},{7,23},{8,24},{9,... | collective-permute-start | bytes 36872 | tf_op jit(solution)/shard_map/ppermute | solution.py:411
  58.5 4.0 %collective-permute-start.13 = (f32[24,128]{1,0:T(8,128)S(1)}, f32[24,128]{1,0:T(8,128)S(1)}, u32[]{:S(2)}, u32[]{:S(2)}) collective-permute-start(f32[24,128]{1,0:T(8,128)S(1)} %get-tuple-element.97.refs_0_), channel_id=1, source_target_pairs={{0,8},{1,9},{2,10},{3,11},{4,12},{5,13},{6,14},{7,15},{8,0},{9,1},... | collective-permute-start | bytes 36872 | tf_op jit(solution)/shard_map/ppermute | solution.py:411

commit v2 on v1

--- a/solution.py
+++ b/solution.py
@@ -13,7 +13,8 @@
 SM = pl.BlockSpec(memory_space=pltpu.SMEM)
 MIB = 2**20
 LANES = 128
-HELD_BYTES = 16 * MIB
+HELD_BYTES = 20 * MIB
+SUB = 32
 LAG = 2
 NO_LABEL = -4.0e6
 SCOPED = 4 * MIB
@@ -156,14 +157,20 @@
     msg_ref, w_ref, logits_ref, x_ref, acc_ref, acc_sem, x_sem = refs
     rows, width = w_ref.shape[0], 2 * LANES
     columns = pl.ds(k * width, width)
+    if k == 0:
+        copy = pltpu.make_async_copy(blocks[0], x_ref.at[pl.ds(LANES, LANES)], x_sem)
+        copy.start()
     accum_copy = None
     if held[1] > held[0]:
         part = pl.ds(held[0], held[1] - held[0])
         accum_copy = pltpu.make_async_copy(accum_hbm.at[part], acc_ref.at[part], acc_sem)
-        accum_copy.start()
+
+        def start(_, carry):
+            accum_copy.start()
+            return carry
+
+        lax.fori_loop(0, jnp.minimum(lax.axis_index("blk") + 1, 1), start, 0)
     if k == 0:
-        copy = pltpu.make_async_copy(blocks[0], x_ref.at[pl.ds(LANES, LANES)], x_sem)
-        copy.start()
         copy.wait()
     else:
         at = k * width
@@ -259,7 +266,7 @@
     msgs, refs = refs[:n_msgs], refs[n_msgs:]
     other_ref, accum_hbm, logits_ref, x_ref = refs[:4]
     w_ref, acc_ref, out_w, out_acc, out_lse = refs[6:11]
-    canon_s, lse_s, label_s, delta_s, read_sem, acc_sem, w_sem = refs[11:]
+    canon_s, lse_s, label_s, delta_s, grad_s, read_sem, acc_sem, w_sem = refs[11:]
     rows, batch = logits_ref.shape
     feats = x_ref.shape[1]
     blocks = rows // bm
@@ -321,15 +328,29 @@
             read(i).wait()
 
         make_delta(jnp.minimum(i + 1, blocks - 1), 1 - now)
-        for n in range(feats // bn):
+        def grad_tile(n):
+            grad_s[n % 2] = jnp.dot(
+                delta_s[now], x_ref[:, pl.ds(n * bn, bn)], preferred_element_type=f32
+            )
+
+        def update_tile(n):
             cols = pl.ds(n * bn, bn)
-            grad = jnp.dot(delta_s[now], x_ref[:, cols], preferred_element_type=f32)
-            new_acc = acc_ref[rows_of(slot), cols] + grad * grad
-            acc_ref[rows_of(slot), cols] = new_acc
-            old = w_ref[rows_of(i), cols].astype(f32)
-            w_ref[rows_of(i), cols] = (
-                old - 0.05 * grad / (jnp.sqrt(new_acc) + 1e-10)
-            ).astype(bf16)
+            for r in range(0, bm, SUB):
+                a_rows = pl.ds(pl.multiple_of(slot * bm + r, SUB), SUB)
+                w_rows = pl.ds(pl.multiple_of(i * bm + r, SUB), SUB)
+                grad = grad_s[n % 2, pl.ds(r, SUB), :]
+                new_acc = acc_ref[a_rows, cols] + grad * grad
+                acc_ref[a_rows, cols] = new_acc
+                root = new_acc * lax.rsqrt(new_acc)
+                part = (0.05 * grad) * pltpu.reciprocal(root + 1e-10, approx=True)
+                w_ref[w_rows, cols] = (w_ref[w_rows, cols].astype(f32) - part).astype(bf16)
+
+        tiles = feats // bn
+        grad_tile(0)
+        for n in range(1, tiles):
+            grad_tile(n)
+            update_tile(n - 1)
+        update_tile(tiles - 1)
 
         @pl.when(i >= LAG)
         def _():
@@ -354,7 +375,7 @@
     rows, batch = logits.shape
     feats = x.shape[1]
     held_blocks = acc_v.shape[0] // bm
-    bn = min(512, feats)
+    bn = min(256, feats)
     inputs = [in_vmem(m) for m in msgs] + [other, in_hbm(accum)] + [
         in_vmem(a) for a in (logits, x, weight_v, acc_v)
     ]
@@ -378,6 +399,7 @@
             pltpu.VMEM((1, batch), f32),
             pltpu.VMEM((1, batch), i32),
             pltpu.VMEM((2, bm, batch), bf16),
+            pltpu.VMEM((2, bm, bn), f32),
             pltpu.SemaphoreType.DMA((held_blocks,)),
             pltpu.SemaphoreType.DMA((held_blocks,)),
             pltpu.SemaphoreType.DMA((LAG + 1,)),
@@ -441,7 +463,7 @@
             if k == steps - 2:
                 came, state[1:] = small_call(head_kernel, "head", (block, feats), [came], state[1:])
             came = round_ring(came)
-        cut = [min(held_rows, held_rows * i // 2) for i in (k, k + 1)] if k < 2 else [0, 0]
+        cut = [bm * min(held_rows // bm, 4 * i) for i in (k, k + 1)]
         state = list(score(k, chips, blocks, accum, tuple(cut), state))
         if k < steps - 1:
             came, state[0] = lax.optimization_barrier((came, state[0]))

time: 102 us -> 92.6 us (0.908)
  Pallas kernels: 72.2 us -> 58.6 us
  waiting for transfers between devices: 9.05 us -> 13 us
    pallas_call x1, Pallas kernels: 39.1 us -> 31.1 us  [update(): pl.pallas_call(functools.partial(update_kernel, cfg), name='update', out_...]
    pallas_call x4, Pallas kernels: 27 us -> 21.4 us  [score(): pl.pallas_call(functools.partial(score_kernel, cfg), name=f'score_{k}', o...]
    ppermute x4, waiting for transfers between devices: 0.36 us -> 3.34 us  [round_ring(): return lax.ppermute(x, 'blk', ring_pairs(chips))]
    ppermute x7, waiting for transfers between devices: 6.75 us -> 7.92 us  [exchange_stats(): messages.append(lax.ppermute(message, ('blk', 'cls'), pairs))]
  transfers between devices with their start and end apart: 16 -> 16, of which waited for: 9 -> 11; matrix products, arithmetic and copies ran while one was open for 1% -> 1% of each run, Pallas kernels for 28% -> 24%
where the time goes in v2:
time: 92.6 us; the launch traced here: 92.4 us
  Pallas kernels  58.6 us (63%)
  starting transfers between devices  18.3 us (20%)
  waiting for transfers between devices  13 us (14%)
  between operations  1.53 us (2%)
  local copies, waits for them, and re-layouts  0.99 us (1%)
    pallas_call x1, Pallas kernels, update(): pl.pallas_call(functools.partial(update_kernel, cfg), name='update', out_...  31.1 us
    pallas_call x4, Pallas kernels, score(): pl.pallas_call(functools.partial(score_kernel, cfg), name=f'score_{k}', o...  21.4 us
    ppermute x4, starting transfers between devices, round_ring(): return lax.ppermute(x, 'blk', ring_pairs(chips))  9.28 us
    ppermute x7, starting transfers between devices, exchange_stats(): messages.append(lax.ppermute(message, ('blk', 'cls'), pairs))  8.23 us
    ppermute x7, waiting for transfers between devices, exchange_stats(): messages.append(lax.ppermute(message, ('blk', 'cls'), pairs))  7.92 us
    pallas_call x1, Pallas kernels, hold(): pl.pallas_call(functools.partial(hold_kernel, chips, pieces), name='hold_...  6.08 us
    ppermute x4, waiting for transfers between devices, round_ring(): return lax.ppermute(x, 'blk', ring_pairs(chips))  3.34 us
  transfers between devices with their start and end apart: 16, of which 11 were waited for; matrix products, arithmetic and copies ran while one was open for 1% of the time, Pallas kernels for 24%

profile of v2, /device:TPU:0, one launch (start us, length us, event | category | flops | bytes accessed | tf_op | source)
XLA Modules:
  0.0 92.4 jit_solution(7892644665745225269)
XLA Ops:
  0.6 0.5 collective-permute-start
  1.1 1.0 %constant_dynamic-update-slice_fusion.1 = bf16[128,2048]{1,0:T(8,128)(2,1)S(1)} fusion(bf16[64,2048]{1,0:T(8,128)(2,1)} %param.6), kind=kLoop, calls=%fused_computation.1 | loop fusion | bytes 524288
  2.1 0.4 collective-permute-done
  2.5 0.0 copy-start
  2.6 3.0 %collective-permute-start.1 = (bf16[128,2048]{1,0:T(8,128)(2,1)S(1)}, bf16[128,2048]{1,0:T(8,128)(2,1)S(1)}, u32[]{:S(2)}, u32[]{:S(2)}) collective-permute-start(bf16[128,2048]{1,0:T(8,128)(2,1)S(1)} %constant_dynamic-update-slice_fusion.pair_hbm), channel_id=1, source_target_pairs={{0,8},{2,6},{8,16},{10,2},{16,24},{18,10},{24,28},{26,18},{28,20},... | collective-permute-start | bytes 1572872 | tf_op jit(solution)/shard_map/ppermute | solution.py:451
  6.2 0.0 copy-done
  6.2 6.1 %hold_weight.1 = (bf16[4096,2048]{1,0:T(8,128)(2,1)S(1)}, f32[4096,1024]{1,0:T(8,128)S(1)}, bf16[1024,2048]{1,0:T(8,128)(2,1)S(1)}, f32[2560,2048]{1,0:T(8,128)S(1)}, f32[24,128]{1,0:T(8,128)S(1)}) custom-call(bf16[4096,2048]{1,0:T(8,128)(2,1)} %w_hbm.1, bf16[128,2048]{1,0:T(8,128)(2,1)} %copy-done, s32[1,64]{1,0:T(1,128)} %bitcast.4, s32[1]{0:T(128)S(6)} %copy.70.offset_ref), custom_call_target="tpu_custom_call" | custom-call | bytes 16777216 | tf_op jit(solution)/shard_map/hold_weight/pallas_call | solution.py:118
  12.3 0.4 collective-permute-done.1.refs_0_
  12.7 0.0 copy-start.1
  12.7 2.1 %collective-permute-start.2 = (bf16[128,2048]{1,0:T(8,128)(2,1)S(1)}, bf16[128,2048]{1,0:T(8,128)(2,1)S(1)}, u32[]{:S(2)}, u32[]{:S(2)}) collective-permute-start(bf16[128,2048]{1,0:T(8,128)(2,1)S(1)} %collective-permute-done.1.refs_0_), channel_id=1, source_target_pairs={{0,8},{2,6},{8,16},{10,2},{16,24},{18,10},{24,28},{26,18},{28,20},... | collective-permute-start | bytes 1572872 | tf_op jit(solution)/shard_map/ppermute | solution.py:451
  14.7 0.0 collective-permute-start.4
  14.7 0.0 copy-done.1
  14.7 6.1 %score_0.1 = (f32[24,128]{1,0:T(8,128)S(1)}, bf16[4096,2048]{1,0:T(8,128)(2,1)S(1)}, f32[4096,1024]{1,0:T(8,128)S(1)}, bf16[1024,2048]{1,0:T(8,128)(2,1)S(1)}, f32[2560,2048]{1,0:T(8,128)S(1)}) custom-call(bf16[128,2048]{1,0:T(8,128)(2,1)} %copy-done.1, ...), custom_call_target="tpu_custom_call", output_to_operand_aliasing={{1}: (3, {}), {2}: (4, {}), {3}: (5, {}), {4}: (6, {})} | custom-call | flops 4294967296 | bytes 17825792 | tf_op jit(solution)/shard_map/score_0/pallas_call | solution.py:216
  20.9 1.0 %collective-permute-done.2.refs_1_ = bf16[128,2048]{1,0:T(8,128)(2,1)S(1)} collective-permute-done((bf16[128,2048]{1,0:T(8,128)(2,1)S(1)}, bf16[128,2048]{1,0:T(8,128)(2,1)S(1)}, u32[]{:S(2)}, u32[]{:S(2)}) %collective-permute-start.2) | collective-permute-done | bytes 524320 | tf_op jit(solution)/shard_map/ppermute | solution.py:451
  21.8 2.1 %collective-permute-start.3 = (bf16[128,2048]{1,0:T(8,128)(2,1)S(1)}, bf16[128,2048]{1,0:T(8,128)(2,1)S(1)}, u32[]{:S(2)}, u32[]{:S(2)}) collective-permute-start(bf16[128,2048]{1,0:T(8,128)(2,1)S(1)} %collective-permute-done.2.refs_1_), channel_id=1, source_target_pairs={{0,8},{2,6},{8,16},{10,2},{16,24},{18,10},{24,28},{26,18},{28,20},... | collective-permute-start | bytes 1572872 | tf_op jit(solution)/shard_map/ppermute | solution.py:451
  23.9 0.0 collective-permute-start.7
  23.9 0.0 collective-permute-done.4.refs_0_
  23.9 5.1 %score_1.1 = (f32[24,128]{1,0:T(8,128)S(1)}, bf16[4096,2048]{1,0:T(8,128)(2,1)S(1)}, f32[4096,1024]{1,0:T(8,128)S(1)}, bf16[1024,2048]{1,0:T(8,128)(2,1)S(1)}, f32[2560,2048]{1,0:T(8,128)S(1)}) custom-call(bf16[128,2048]{1,0:T(8,128)(2,1)S(1)} %collective-permute-done.4.refs_0_, ...), custom_call_target="tpu_custom_call", output_to_operand_aliasing={{1}: (4, {}), {2}: (5, {}), {3}: (6, {}), {4}: (7, {})} | custom-call | flops 4294967296 | bytes 17825792 | tf_op jit(solution)/shard_map/score_1/pallas_call | solution.py:216
  29.0 2.0 %collective-permute-done.3.refs_0_.refs_1_ = bf16[128,2048]{1,0:T(8,128)(2,1)S(1)} collective-permute-done((bf16[128,2048]{1,0:T(8,128)(2,1)S(1)}, bf16[128,2048]{1,0:T(8,128)(2,1)S(1)}, u32[]{:S(2)}, u32[]{:S(2)}) %collective-permute-start.3) | collective-permute-done | bytes 524320 | tf_op jit(solution)/shard_map/ppermute | solution.py:451
  31.0 0.0 collective-permute-start.5
  31.0 2.1 %collective-permute-start.6 = (bf16[64,2048]{1,0:T(8,128)(2,1)S(1)}, bf16[64,2048]{1,0:T(8,128)(2,1)S(1)}, u32[]{:S(2)}, u32[]{:S(2)}) collective-permute-start(bf16[64,2048]{1,0:T(8,128)(2,1)S(1)} %get-tuple-element.74), channel_id=1, source_target_pairs={{0,8},{2,6},{8,16},{10,2},{16,24},{18,10},{24,28},{26,18},{28,20},... | collective-permute-start | bytes 786440 | tf_op jit(solution)/shard_map/ppermute | solution.py:451
  33.2 0.0 collective-permute-done.7.refs_0_
  33.2 5.1 %score_2.1 = (f32[24,128]{1,0:T(8,128)S(1)}, bf16[4096,2048]{1,0:T(8,128)(2,1)S(1)}, f32[4096,1024]{1,0:T(8,128)S(1)}, bf16[1024,2048]{1,0:T(8,128)(2,1)S(1)}, f32[2560,2048]{1,0:T(8,128)S(1)}) custom-call(bf16[128,2048]{1,0:T(8,128)(2,1)S(1)} %collective-permute-done.7.refs_0_, ...), custom_call_target="tpu_custom_call", output_to_operand_aliasing={{1}: (4, {}), {2}: (5, {}), {3}: (6, {}), {4}: (7, {})} | custom-call | flops 4294967296 | bytes 17825792 | tf_op jit(solution)/shard_map/score_2/pallas_call | solution.py:216
  38.3 0.0 collective-permute-done.6.refs_1_
  38.3 0.2 collective-permute-start.8
  38.5 1.4 %collective-permute-done.8.refs_2_ = bf16[64,2048]{1,0:T(8,128)(2,1)S(1)} collective-permute-done((bf16[64,2048]{1,0:T(8,128)(2,1)S(1)}, bf16[64,2048]{1,0:T(8,128)(2,1)S(1)}, u32[]{:S(2)}, u32[]{:S(2)}) %collective-permute-start.8) | collective-permute-done | bytes 262176 | tf_op jit(solution)/shard_map/ppermute | solution.py:448
  39.9 0.0 collective-permute-done.5.refs_0_
  39.9 5.1 %score_3.1 = (f32[24,128]{1,0:T(8,128)S(1)}, bf16[4096,2048]{1,0:T(8,128)(2,1)S(1)}, f32[4096,1024]{1,0:T(8,128)S(1)}, bf16[1024,2048]{1,0:T(8,128)(2,1)S(1)}, f32[2560,2048]{1,0:T(8,128)S(1)}) custom-call(bf16[128,2048]{1,0:T(8,128)(2,1)S(1)} %collective-permute-done.5.refs_0_, ...), custom_call_target="tpu_custom_call", output_to_operand_aliasing={{1}: (5, {}), {2}: (6, {}), {3}: (7, {}), {4}: (8, {})} | custom-call | flops 4294967296 | bytes 17825792 | tf_op jit(solution)/shard_map/score_3/pallas_call | solution.py:216
  45.0 0.2 collective-permute-start.9
  45.2 1.0 %collective-permute-done.9.refs_1_ = f32[24,128]{1,0:T(8,128)S(1)} collective-permute-done((f32[24,128]{1,0:T(8,128)S(1)}, f32[24,128]{1,0:T(8,128)S(1)}, u32[]{:S(2)}, u32[]{:S(2)}) %collective-permute-start.9) | collective-permute-done | bytes 12320 | tf_op jit(solution)/shard_map/ppermute | solution.py:433
  46.2 2.4 %collective-permute-start.12 = (f32[24,128]{1,0:T(8,128)S(1)}, f32[24,128]{1,0:T(8,128)S(1)}, u32[]{:S(2)}, u32[]{:S(2)}) collective-permute-start(f32[24,128]{1,0:T(8,128)S(1)} %get-tuple-element.92.refs_0_), channel_id=1, source_target_pairs={{0,5},{1,4},{2,7},{3,6},{4,1},{5,0},{6,3},{7,2},{8,13},{9,12},{10,... | collective-permute-start | bytes 36872 | tf_op jit(solution)/shard_map/ppermute | solution.py:433
  48.6 0.6 collective-permute-start.11
  49.3 0.5 collective-permute-start.10
  49.8 1.1 %collective-permute-done.12.refs_3_ = f32[24,128]{1,0:T(8,128)S(1)} collective-permute-done((f32[24,128]{1,0:T(8,128)S(1)}, f32[24,128]{1,0:T(8,128)S(1)}, u32[]{:S(2)}, u32[]{:S(2)}) %collective-permute-start.12) | collective-permute-done | bytes 12320 | tf_op jit(solution)/shard_map/ppermute | solution.py:433
  50.9 1.4 %collective-permute-done.11.refs_2_ = f32[24,128]{1,0:T(8,128)S(1)} collective-permute-done((f32[24,128]{1,0:T(8,128)S(1)}, f32[24,128]{1,0:T(8,128)S(1)}, u32[]{:S(2)}, u32[]{:S(2)}) %collective-permute-start.11) | collective-permute-done | bytes 12320 | tf_op jit(solution)/shard_map/ppermute | solution.py:433
  52.3 0.6 collective-permute-done.10.refs_1_
  53.0 3.6 %collective-permute-start.15 = (f32[24,128]{1,0:T(8,128)S(1)}, f32[24,128]{1,0:T(8,128)S(1)}, u32[]{:S(2)}, u32[]{:S(2)}) collective-permute-start(f32[24,128]{1,0:T(8,128)S(1)} %get-tuple-element.97.refs_0_), channel_id=1, source_target_pairs={{0,24},{1,25},{2,26},{3,27},{4,28},{5,29},{6,30},{7,31},{8,16},{9,... | collective-permute-start | bytes 36872 | tf_op jit(solution)/shard_map/ppermute | solution.py:433
  56.6 0.0 collective-permute-start.14
  56.6 0.8 collective-permute-start.13
  57.4 1.1 %collective-permute-done.15.refs_3_ = f32[24,128]{1,0:T(8,128)S(1)} collective-permute-done((f32[24,128]{1,0:T(8,128)S(1)}, f32[24,128]{1,0:T(8,128)S(1)}, u32[]{:S(2)}, u32[]{:S(2)}) %collective-permute-start.15) | collective-permute-done | bytes 12320 | tf_op jit(solution)/shard_map/ppermute | solution.py:433
  58.5 2.6 %collective-permute-done.14.refs_2_ = f32[24,128]{1,0:T(8,128)S(1)} collective-permute-done((f32[24,128]{1,0:T(8,128)S(1)}, f32[24,128]{1,0:T(8,128)S(1)}, u32[]{:S(2)}, u32[]{:S(2)}) %collective-permute-start.14) | collective-permute-done | bytes 12320 | tf_op jit(solution)/shard_map/ppermute | solution.py:433
  61.2 0.0 collective-permute-done.13.refs_1_
  61.2 31.1 %update.1 = (bf16[4096,2048]{1,0:T(8,128)(2,1)S(1)}, f32[2560,2048]{1,0:T(8,128)S(1)}, bf16[4096,2048]{1,0:T(8,128)(2,1)}, f32[4096,2048]{1,0:T(8,128)}, f32[1,64]{1,0:T(1,128)}) custom-call(f32[24,128]{1,0:T(8,128)S(1)} %get-tuple-element.97.refs_0_, f32[24,128]{1,0:T(8,128)S(1)} %collective-permute-done.13.refs_1_, ...), custom_call_target="tpu_custom_call", output_to_operand_aliasing={{0}: (8, {}), {1}: (9, {})} | custom-call | flops 17179869184 | bytes 83886080 | tf_op jit(solution)/shard_map/update/pallas_call | solution.py:384
  (4 shorter events, 0.1 us)
Async XLA Ops:
  0.6 1.9 %collective-permute-start = (bf16[64,2048]{1,0:T(8,128)(2,1)}, bf16[64,2048]{1,0:T(8,128)(2,1)S(1)}, u32[]{:S(2)}, u32[]{:S(2)}) collective-permute-start(bf16[64,2048]{1,0:T(8,128)(2,1)} %param.6), channel_id=1, source_target_pairs={{0,2},{2,0},{4,6},{6,4},{8,10},{10,8},{12,14},{14,12},{16,18},{18,... | collective-permute-start | bytes 786440 | tf_op jit(solution)/shard_map/ppermute | solution.py:448
  2.5 3.7 %copy-start = (bf16[128,2048]{1,0:T(8,128)(2,1)}, bf16[128,2048]{1,0:T(8,128)(2,1)S(1)}, u32[]{:S(2)}) copy-start(bf16[128,2048]{1,0:T(8,128)(2,1)S(1)} %constant_dynamic-update-slice_fusion.pair_hbm) | copy-start | bytes 1572868
  2.6 10.1 %collective-permute-start.1 = (bf16[128,2048]{1,0:T(8,128)(2,1)S(1)}, bf16[128,2048]{1,0:T(8,128)(2,1)S(1)}, u32[]{:S(2)}, u32[]{:S(2)}) collective-permute-start(bf16[128,2048]{1,0:T(8,128)(2,1)S(1)} %constant_dynamic-update-slice_fusion.pair_hbm), channel_id=1, source_target_pairs={{0,8},{2,6},{8,16},{10,2},{16,24},{18,10},{24,28},{26,18},{28,20},... | collective-permute-start | bytes 1572872 | tf_op jit(solution)/shard_map/ppermute | solution.py:451
  12.7 2.1 %copy-start.1 = (bf16[128,2048]{1,0:T(8,128)(2,1)}, bf16[128,2048]{1,0:T(8,128)(2,1)S(1)}, u32[]{:S(2)}) copy-start(bf16[128,2048]{1,0:T(8,128)(2,1)S(1)} %collective-permute-done.1.refs_0_) | copy-start | bytes 1572868
  12.7 9.2 %collective-permute-start.2 = (bf16[128,2048]{1,0:T(8,128)(2,1)S(1)}, bf16[128,2048]{1,0:T(8,128)(2,1)S(1)}, u32[]{:S(2)}, u32[]{:S(2)}) collective-permute-start(bf16[128,2048]{1,0:T(8,128)(2,1)S(1)} %collective-permute-done.1.refs_0_), channel_id=1, source_target_pairs={{0,8},{2,6},{8,16},{10,2},{16,24},{18,10},{24,28},{26,18},{28,20},... | collective-permute-start | bytes 1572872 | tf_op jit(solution)/shard_map/ppermute | solution.py:451
  14.7 9.2 %collective-permute-start.4 = (bf16[128,2048]{1,0:T(8,128)(2,1)S(1)}, bf16[128,2048]{1,0:T(8,128)(2,1)S(1)}, u32[]{:S(2)}, u32[]{:S(2)}) collective-permute-start(bf16[128,2048]{1,0:T(8,128)(2,1)S(1)} %collective-permute-done.1.refs_0_), channel_id=1, source_target_pairs={{0,2},{2,0},{4,6},{6,4},{8,10},{10,8},{12,14},{14,12},{16,18},{18,... | collective-permute-start | bytes 1572872 | tf_op jit(solution)/shard_map/ppermute | solution.py:448
  21.8 9.2 %collective-permute-start.3 = (bf16[128,2048]{1,0:T(8,128)(2,1)S(1)}, bf16[128,2048]{1,0:T(8,128)(2,1)S(1)}, u32[]{:S(2)}, u32[]{:S(2)}) collective-permute-start(bf16[128,2048]{1,0:T(8,128)(2,1)S(1)} %collective-permute-done.2.refs_1_), channel_id=1, source_target_pairs={{0,8},{2,6},{8,16},{10,2},{16,24},{18,10},{24,28},{26,18},{28,20},... | collective-permute-start | bytes 1572872 | tf_op jit(solution)/shard_map/ppermute | solution.py:451
  23.9 9.3 %collective-permute-start.7 = (bf16[128,2048]{1,0:T(8,128)(2,1)S(1)}, bf16[128,2048]{1,0:T(8,128)(2,1)S(1)}, u32[]{:S(2)}, u32[]{:S(2)}) collective-permute-start(bf16[128,2048]{1,0:T(8,128)(2,1)S(1)} %collective-permute-done.2.refs_1_), channel_id=1, source_target_pairs={{0,2},{2,0},{4,6},{6,4},{8,10},{10,8},{12,14},{14,12},{16,18},{18,... | collective-permute-start | bytes 1572872 | tf_op jit(solution)/shard_map/ppermute | solution.py:448
  31.0 8.9 %collective-permute-start.5 = (bf16[128,2048]{1,0:T(8,128)(2,1)S(1)}, bf16[128,2048]{1,0:T(8,128)(2,1)S(1)}, u32[]{:S(2)}, u32[]{:S(2)}) collective-permute-start(bf16[128,2048]{1,0:T(8,128)(2,1)S(1)} %collective-permute-done.3.refs_0_.refs_1_), channel_id=1, source_target_pairs={{0,2},{2,0},{4,6},{6,4},{8,10},{10,8},{12,14},{14,12},{16,18},{18,... | collective-permute-start | bytes 1572872 | tf_op jit(solution)/shard_map/ppermute | solution.py:448
  31.0 7.2 %collective-permute-start.6 = (bf16[64,2048]{1,0:T(8,128)(2,1)S(1)}, bf16[64,2048]{1,0:T(8,128)(2,1)S(1)}, u32[]{:S(2)}, u32[]{:S(2)}) collective-permute-start(bf16[64,2048]{1,0:T(8,128)(2,1)S(1)} %get-tuple-element.74), channel_id=1, source_target_pairs={{0,8},{2,6},{8,16},{10,2},{16,24},{18,10},{24,28},{26,18},{28,20},... | collective-permute-start | bytes 786440 | tf_op jit(solution)/shard_map/ppermute | solution.py:451
  38.3 1.6 %collective-permute-start.8 = (bf16[64,2048]{1,0:T(8,128)(2,1)S(1)}, bf16[64,2048]{1,0:T(8,128)(2,1)S(1)}, u32[]{:S(2)}, u32[]{:S(2)}) collective-permute-start(bf16[64,2048]{1,0:T(8,128)(2,1)S(1)} %collective-permute-done.6.refs_1_), channel_id=1, source_target_pairs={{0,2},{2,0},{4,6},{6,4},{8,10},{10,8},{12,14},{14,12},{16,18},{18,... | collective-permute-start | bytes 786440 | tf_op jit(solution)/shard_map/ppermute | solution.py:448
  45.0 1.2 %collective-permute-start.9 = (f32[24,128]{1,0:T(8,128)S(1)}, f32[24,128]{1,0:T(8,128)S(1)}, u32[]{:S(2)}, u32[]{:S(2)}) collective-permute-start(f32[24,128]{1,0:T(8,128)S(1)} %get-tuple-element.87.refs_0_), channel_id=1, source_target_pairs={{0,2},{1,3},{2,0},{3,1},{4,6},{5,7},{6,4},{7,5},{8,10},{9,11},{10,... | collective-permute-start | bytes 36872 | tf_op jit(solution)/shard_map/ppermute | solution.py:433
  46.2 4.7 %collective-permute-start.12 = (f32[24,128]{1,0:T(8,128)S(1)}, f32[24,128]{1,0:T(8,128)S(1)}, u32[]{:S(2)}, u32[]{:S(2)}) collective-permute-start(f32[24,128]{1,0:T(8,128)S(1)} %get-tuple-element.92.refs_0_), channel_id=1, source_target_pairs={{0,5},{1,4},{2,7},{3,6},{4,1},{5,0},{6,3},{7,2},{8,13},{9,12},{10,... | collective-permute-start | bytes 36872 | tf_op jit(solution)/shard_map/ppermute | solution.py:433
  48.6 3.7 %collective-permute-start.11 = (f32[24,128]{1,0:T(8,128)S(1)}, f32[24,128]{1,0:T(8,128)S(1)}, u32[]{:S(2)}, u32[]{:S(2)}) collective-permute-start(f32[24,128]{1,0:T(8,128)S(1)} %get-tuple-element.92.refs_0_), channel_id=1, source_target_pairs={{0,4},{1,5},{2,6},{3,7},{4,0},{5,1},{6,2},{7,3},{8,12},{9,13},{10,... | collective-permute-start | bytes 36872 | tf_op jit(solution)/shard_map/ppermute | solution.py:433
  49.3 3.7 %collective-permute-start.10 = (f32[24,128]{1,0:T(8,128)S(1)}, f32[24,128]{1,0:T(8,128)S(1)}, u32[]{:S(2)}, u32[]{:S(2)}) collective-permute-start(f32[24,128]{1,0:T(8,128)S(1)} %get-tuple-element.92.refs_0_), channel_id=1, source_target_pairs={{0,1},{1,0},{2,3},{3,2},{4,5},{5,4},{6,7},{7,6},{8,9},{9,8},{10,11... | collective-permute-start | bytes 36872 | tf_op jit(solution)/shard_map/ppermute | solution.py:433
  53.0 5.6 %collective-permute-start.15 = (f32[24,128]{1,0:T(8,128)S(1)}, f32[24,128]{1,0:T(8,128)S(1)}, u32[]{:S(2)}, u32[]{:S(2)}) collective-permute-start(f32[24,128]{1,0:T(8,128)S(1)} %get-tuple-element.97.refs_0_), channel_id=1, source_target_pairs={{0,24},{1,25},{2,26},{3,27},{4,28},{5,29},{6,30},{7,31},{8,16},{9,... | collective-permute-start | bytes 36872 | tf_op jit(solution)/shard_map/ppermute | solution.py:433
  56.6 4.6 %collective-permute-start.14 = (f32[24,128]{1,0:T(8,128)S(1)}, f32[24,128]{1,0:T(8,128)S(1)}, u32[]{:S(2)}, u32[]{:S(2)}) collective-permute-start(f32[24,128]{1,0:T(8,128)S(1)} %get-tuple-element.97.refs_0_), channel_id=1, source_target_pairs={{0,16},{1,17},{2,18},{3,19},{4,20},{5,21},{6,22},{7,23},{8,24},{9,... | collective-permute-start | bytes 36872 | tf_op jit(solution)/shard_map/ppermute | solution.py:433
  56.6 4.6 %collective-permute-start.13 = (f32[24,128]{1,0:T(8,128)S(1)}, f32[24,128]{1,0:T(8,128)S(1)}, u32[]{:S(2)}, u32[]{:S(2)}) collective-permute-start(f32[24,128]{1,0:T(8,128)S(1)} %get-tuple-element.97.refs_0_), channel_id=1, source_target_pairs={{0,8},{1,9},{2,10},{3,11},{4,12},{5,13},{6,14},{7,15},{8,0},{9,1},... | collective-permute-start | bytes 36872 | tf_op jit(solution)/shard_map/ppermute | solution.py:433

commit v3 on v2

--- a/solution.py
+++ b/solution.py
@@ -13,6 +13,7 @@
 SM = pl.BlockSpec(memory_space=pltpu.SMEM)
 MIB = 2**20
 LANES = 128
+PIECES = 2
 HELD_BYTES = 20 * MIB
 SUB = 32
 LAG = 2
@@ -55,21 +56,20 @@
     return chip, core, place
 
 
-def pair_slots(chips):
+def block_slots(chips):
     _, core, place = whereabouts(chips)
     sign = 1 - 2 * core
-    slots = [(chip_at(place, chips), core)]
-    for step in range(1, chips // 2):
-        slots.append((chip_at(place - step * sign, chips), core))
-        slots.append((chip_at(place + step * sign, chips), 1 - core))
-    slots.append((chip_at(place + chips // 2, chips), core))
-    return slots
-
-
-def swapped(row, swap):
+    slots = [(place, core), (place, 1 - core), (place - sign, core), (place + sign, 1 - core)]
+    for step in range(2, chips // 2 + 1):
+        near, far = (step - 1) * sign, step * sign
+        slots += [(place - near, 1 - core), (place - far, core)]
+        slots += [(place + near, core), (place + far, 1 - core)]
+    return [(chip_at(at, chips), side) for at, side in slots]
+
+
+def one_half(row, side):
     half = row.shape[1] // 2
-    other = jnp.concatenate([row[:, half:], row[:, :half]], axis=1)
-    return jnp.where(swap == 1, other, row)
+    return jnp.where(side == 0, row[:, :half], row[:, half:])
 
 
 def merge_parts(messages):
@@ -80,21 +80,25 @@
     return top, total, functools.reduce(jnp.maximum, [m[2 * n :] for m in messages])
 
 
-def hold_kernel(chips, pieces, w_hbm, pair_hbm, labels_hbm, offset_ref, *refs):
-    w_ref, _, x_ref, _, msg_ref, labels_ref, sem, pair_sem, label_sem = refs
-    rows = w_ref.shape[0] // pieces
-    copies = [
+def weight_copies(w_hbm, w_ref, sem, half):
+    pieces = sem.shape[0]
+    rows = w_ref.shape[0] // 2 // pieces
+    first = half * pieces
+    return [
         pltpu.make_async_copy(
-            w_hbm.at[pl.ds(i * rows, rows)], w_ref.at[pl.ds(i * rows, rows)], sem.at[i]
+            w_hbm.at[pl.ds((first + i) * rows, rows)],
+            w_ref.at[pl.ds((first + i) * rows, rows)],
+            sem.at[i],
         )
         for i in range(pieces)
     ]
+
+
+def hold_kernel(chips, w_hbm, labels_hbm, offset_ref, *refs):
+    w_ref, _, _, _, msg_ref, labels_ref, sem, label_sem = refs
+    copies = weight_copies(w_hbm, w_ref, sem, 0)
     label_copy = pltpu.make_async_copy(labels_hbm, labels_ref, label_sem)
     label_copy.start()
-    pair_copy = pltpu.make_async_copy(
-        pair_hbm, x_ref.at[pl.ds(0, pair_hbm.shape[0])], pair_sem
-    )
-    pair_copy.start()
     for copy in copies:
         copy.start()
     label_copy.wait()
@@ -108,15 +112,13 @@
     )
     for copy in copies:
         copy.wait()
-    pair_copy.wait()
-
-
-def hold(weight, pair, labels, offset, chips, batch, held_rows):
-    pieces = 4
+
+
+def hold(weight, labels, offset, chips, batch, held_rows):
     rows, feats = weight.shape
     labels = labels.reshape(1, -1)
     return pl.pallas_call(
-        functools.partial(hold_kernel, chips, pieces),
+        functools.partial(hold_kernel, chips),
         name="hold_weight",
         out_shape=[
             pltpu.VMEM((rows, feats), bf16),
@@ -125,19 +127,18 @@
             pltpu.VMEM((held_rows, feats), f32),
             pltpu.VMEM((3 * chips, LANES), f32),
         ],
-        in_specs=[ANY, ANY, ANY, SM],
+        in_specs=[ANY, ANY, SM],
         out_specs=[VM] * 5,
         scratch_shapes=[
             pltpu.VMEM(labels.shape, i32),
-            pltpu.SemaphoreType.DMA((pieces,)),
-            pltpu.SemaphoreType.DMA,
+            pltpu.SemaphoreType.DMA((PIECES,)),
             pltpu.SemaphoreType.DMA,
         ],
         compiler_params=pltpu.CompilerParams(vmem_limit_bytes=SCOPED),
         cost_estimate=pl.CostEstimate(
-            flops=0, bytes_accessed=weight.size * 2, transcendentals=0
+            flops=0, bytes_accessed=weight.size, transcendentals=0
         ),
-    )(in_hbm(weight), in_hbm(pair), in_hbm(labels), offset)
+    )(in_hbm(weight), in_hbm(labels), offset)
 
 
 def fold(op, values):
@@ -152,35 +153,35 @@
 
 def score_kernel(cfg, *refs):
     chips, k, held, bm, n_blocks = cfg
-    blocks, accum_hbm, refs = refs[:n_blocks], refs[n_blocks], refs[n_blocks + 1 :]
+    blocks, accum_hbm, w_hbm, refs = refs[:n_blocks], refs[n_blocks], refs[n_blocks + 1], refs[n_blocks + 2 :]
     msg_in, refs = refs[0], refs[5:]
-    msg_ref, w_ref, logits_ref, x_ref, acc_ref, acc_sem, x_sem = refs
+    msg_ref, w_ref, logits_ref, x_ref, acc_ref, acc_sem, w_sem = refs
     rows, width = w_ref.shape[0], 2 * LANES
     columns = pl.ds(k * width, width)
-    if k == 0:
-        copy = pltpu.make_async_copy(blocks[0], x_ref.at[pl.ds(LANES, LANES)], x_sem)
-        copy.start()
-    accum_copy = None
+    copies = weight_copies(w_hbm, w_ref, w_sem, 1) if k == 0 else []
+    accum_copies = []
     if held[1] > held[0]:
         part = pl.ds(held[0], held[1] - held[0])
-        accum_copy = pltpu.make_async_copy(accum_hbm.at[part], acc_ref.at[part], acc_sem)
-
-        def start(_, carry):
-            accum_copy.start()
-            return carry
-
+        accum_copies = [pltpu.make_async_copy(accum_hbm.at[part], acc_ref.at[part], acc_sem)]
+
+    def start(_, carry):
+        for copy in copies + accum_copies:
+            copy.start()
+        return carry
+
+    if copies + accum_copies:
         lax.fori_loop(0, jnp.minimum(lax.axis_index("blk") + 1, 1), start, 0)
-    if k == 0:
-        copy.wait()
-    else:
-        at = k * width
-        for block in blocks:
-            x_ref[pl.ds(at, block.shape[0]), :] = block[...]
-            at += block.shape[0]
+    at = k * width
+    for block in blocks:
+        x_ref[pl.ds(at, block.shape[0]), :] = block[...]
+        at += block.shape[0]
     x = x_ref.at[columns]
     top = jnp.full((8, width), -3.0e38, f32)
     total = jnp.zeros((8, width), f32)
     for i in range(rows // bm):
+        if i == rows // bm // 2:
+            for copy in copies:
+                copy.wait()
         logits_ref[pl.ds(i * bm, bm), columns] = lax.dot_general(
             w_ref[pl.ds(i * bm, bm), :],
             x[...],
@@ -193,25 +194,27 @@
     one_top = jnp.max(top, axis=0, keepdims=True)
     one_total = jnp.sum(total * jnp.exp(top - one_top), axis=0, keepdims=True)
     msg_ref[...] = msg_in[...]
-    slots = pair_slots(chips)[2 * k : 2 * k + 2]
-    for j, (owner, swap) in enumerate(slots):
-        lanes = slice(j * LANES, (j + 1) * LANES)
-        msg_ref[pl.ds(owner, 1), :] = swapped(one_top[:, lanes], swap)
-        msg_ref[pl.ds(chips + owner, 1), :] = swapped(one_total[:, lanes], swap)
-    if accum_copy is not None:
-        accum_copy.wait()
-
-
-def score(k, chips, blocks, accum, held, state):
+    half = LANES // 2
+    side_of = lax.broadcasted_iota(i32, (1, LANES), 1) // half
+    for j, (owner, side) in enumerate(block_slots(chips)[4 * k : 4 * k + 4]):
+        lanes = slice(j * half, (j + 1) * half)
+        for row, values in ((owner, one_top), (chips + owner, one_total)):
+            twice = jnp.concatenate([values[:, lanes], values[:, lanes]], axis=1)
+            here = pl.ds(row, 1)
+            msg_ref[here, :] = jnp.where(side_of == side, twice, msg_ref[here, :])
+    for copy in accum_copies:
+        copy.wait()
+
+
+def score(k, chips, blocks, accum, weight, held, state):
     rows, feats = state[1].shape
-    bm = min(512, rows)
+    bm = min(512, rows // 2)
     width = 2 * LANES
-    base = len(blocks) + 2
-    place = in_hbm if k == 0 else in_vmem
-    inputs = [place(b) for b in blocks] + [in_hbm(accum)] + [in_vmem(s) for s in state]
-    specs = [ANY if k == 0 else VM] * len(blocks) + [ANY]
+    base = len(blocks) + 3
+    inputs = [in_vmem(b) for b in blocks] + [in_hbm(accum), in_hbm(weight)]
+    inputs += [in_vmem(s) for s in state]
+    specs = [VM] * len(blocks) + [ANY, ANY] + [VM] * len(state)
     aliases = {base + i: 1 + i for i in range(4)}
-    specs += [VM] * (len(inputs) - len(specs))
     cfg = (chips, k, held, bm, len(blocks))
     return pl.pallas_call(
         functools.partial(score_kernel, cfg),
@@ -220,7 +223,7 @@
         in_specs=specs,
         out_specs=[VM] * 5,
         input_output_aliases=aliases,
-        scratch_shapes=[pltpu.SemaphoreType.DMA, pltpu.SemaphoreType.DMA],
+        scratch_shapes=[pltpu.SemaphoreType.DMA, pltpu.SemaphoreType.DMA((PIECES,))],
         compiler_params=pltpu.CompilerParams(vmem_limit_bytes=SCOPED),
         cost_estimate=pl.CostEstimate(
             flops=2 * rows * feats * width,
@@ -249,8 +252,10 @@
     return out, pinned
 
 
-def head_kernel(x_ref, out_ref):
-    out_ref[...] = x_ref[: out_ref.shape[0], :]
+def join_kernel(first_ref, second_ref, out_ref):
+    n = first_ref.shape[0]
+    out_ref[:n] = first_ref[...]
+    out_ref[n:] = second_ref[...]
 
 
 def merge_kernel(*refs):
@@ -283,12 +288,17 @@
     canon_s[chips:] = labels
     own = canon_s[pl.ds(chip, 1), :]
     out_lse[...] = jnp.where(core == 0, own[:, : LANES // 2], own[:, LANES // 2 :])
-    for j, (owner, swap) in enumerate(pair_slots(chips)):
+    slots = block_slots(chips)
+    for j in range(chips):
         lanes = pl.ds(j * LANES, LANES)
-        lse_s[:, lanes] = swapped(canon_s[pl.ds(owner, 1), :], swap)
-        label_s[:, lanes] = (
-            swapped(canon_s[pl.ds(chips + owner, 1), :], swap).astype(i32) - first_class
+        pair = slots[2 * j : 2 * j + 2]
+        lse_s[:, lanes] = jnp.concatenate(
+            [one_half(canon_s[pl.ds(owner, 1), :], side) for owner, side in pair], axis=1
         )
+        label = jnp.concatenate(
+            [one_half(canon_s[pl.ds(chips + owner, 1), :], side) for owner, side in pair], axis=1
+        )
+        label_s[:, lanes] = label.astype(i32) - first_class
 
     def make_delta(i, to):
         r0 = pl.multiple_of(i * bm, bm)
@@ -318,6 +328,7 @@
         )
 
     make_delta(0, 0)
+    grad_s[...] = jnp.zeros_like(grad_s)
 
     def step(i, carry):
         now = lax.rem(i, 2)
@@ -450,24 +461,27 @@
     def round_ring(x):
         return lax.ppermute(x, "blk", ring_pairs(chips))
 
+    came = round_ring(features)
     sibling = swap_cores(features)
-    pair = jnp.concatenate([features, sibling], axis=0)
-    came = round_ring(pair)
-    *pinned, message = hold(weight, pair, labels, offset, chips, batch, held_rows)
+    *pinned, message = hold(weight, labels, offset, chips, batch, held_rows)
+    came, message = lax.optimization_barrier((came, message))
     state = [message, *pinned]
-    came, state[0] = lax.optimization_barrier((came, state[0]))
-    blocks = [came]
+    joined, state[1:] = small_call(
+        join_kernel, "join", (2 * block, feats), [sibling, came], state[1:]
+    )
+    blocks = [features, sibling, came, swap_cores(came)]
+    came = round_ring(joined)
+    held = 0
     for k in range(steps):
-        if k < steps - 1:
-            crossed = swap_cores(came)
-            if k == steps - 2:
-                came, state[1:] = small_call(head_kernel, "head", (block, feats), [came], state[1:])
-            came = round_ring(came)
-        cut = [bm * min(held_rows // bm, 4 * i) for i in (k, k + 1)]
-        state = list(score(k, chips, blocks, accum, tuple(cut), state))
+        if k > 0:
+            blocks = [came, swap_cores(came)]
+            if k < steps - 1:
+                came = round_ring(came)
+        until = held_rows if k == steps - 1 else min(held_rows, 4 * k * bm)
+        state = list(score(k, chips, blocks, accum, weight, (held, until), state))
+        held = until
         if k < steps - 1:
             came, state[0] = lax.optimization_barrier((came, state[0]))
-            blocks = [crossed, came] + ([swap_cores(came)] if k == steps - 2 else [])
     messages, pinned = exchange_stats(state[0], state[1:], blk_size, cls_size)
     weight_v, logits, x, acc_v = pinned
     new_weight, new_accum, lse = update(

time: 92.6 us -> 90 us (0.972)
  Pallas kernels: 58.6 us -> 55.2 us
  waiting for transfers between devices: 13 us -> 16 us
  starting transfers between devices: 18.3 us -> 17.1 us
  local copies, waits for them, and re-layouts: 0.99 us -> 0.01 us
    pallas_call x1, Pallas kernels: 6.08 us -> 3.51 us  [hold(): pl.pallas_call(functools.partial(hold_kernel, chips), name='hold_weight',...]
    ppermute x4, waiting for transfers between devices: 3.34 us -> 5.66 us  [round_ring(): return lax.ppermute(x, 'blk', ring_pairs(chips))]
    pallas_call x1, Pallas kernels: 31.1 us -> 30 us  [update(): pl.pallas_call(functools.partial(update_kernel, cfg), name='update', out_...]
    unnamed x5 -> x2, local copies, waits for them, and re-layouts: 0.98 us -> 0.01 us
  transfers between devices with their start and end apart: 16 -> 16, of which waited for: 11 -> 13; matrix products, arithmetic and copies ran while one was open for 1% -> 0% of each run, Pallas kernels for 24% -> 22%
where the time goes in v3:
time: 90 us; the launch traced here: 89.8 us
  Pallas kernels  55.2 us (61%)
  starting transfers between devices  17.1 us (19%)
  waiting for transfers between devices  16 us (18%)
  between operations  1.51 us (2%)
    pallas_call x1, Pallas kernels, update(): pl.pallas_call(functools.partial(update_kernel, cfg), name='update', out_...  30 us
    pallas_call x4, Pallas kernels, score(): pl.pallas_call(functools.partial(score_kernel, cfg), name=f'score_{k}', o...  21.6 us
    ppermute x4, starting transfers between devices, round_ring(): return lax.ppermute(x, 'blk', ring_pairs(chips))  8.64 us
    ppermute x7, waiting for transfers between devices, exchange_stats(): messages.append(lax.ppermute(message, ('blk', 'cls'), pairs))  8.27 us
    ppermute x7, starting transfers between devices, exchange_stats(): messages.append(lax.ppermute(message, ('blk', 'cls'), pairs))  8.2 us
    ppermute x4, waiting for transfers between devices, round_ring(): return lax.ppermute(x, 'blk', ring_pairs(chips))  5.66 us
    pallas_call x1, Pallas kernels, hold(): pl.pallas_call(functools.partial(hold_kernel, chips), name='hold_weight',...  3.51 us
    ppermute x5, waiting for transfers between devices, swap_cores(): return lax.ppermute(x, 'blk', [(d, d ^ 1) for d in range(blk_size)])  2.05 us
  transfers between devices with their start and end apart: 16, of which 13 were waited for; matrix products, arithmetic and copies ran while one was open for 0% of the time, Pallas kernels for 22%

profile of v3, /device:TPU:0, one launch (start us, length us, event | category | flops | bytes accessed | tf_op | source)
XLA Modules:
  0.0 89.8 jit_solution(7402476017488631385)
XLA Ops:
  0.6 3.1 %collective-permute-start.1 = (bf16[64,2048]{1,0:T(8,128)(2,1)}, bf16[64,2048]{1,0:T(8,128)(2,1)S(1)}, u32[]{:S(2)}, u32[]{:S(2)}) collective-permute-start(bf16[64,2048]{1,0:T(8,128)(2,1)} %refs_0_.1), channel_id=1, source_target_pairs={{0,8},{2,6},{8,16},{10,2},{16,24},{18,10},{24,28},{26,18},{28,20},... | collective-permute-start | bytes 786440 | tf_op jit(solution)/shard_map/ppermute | solution.py:462
  3.7 0.0 collective-permute-start
  4.4 3.5 %hold_weight.1 = (bf16[4096,2048]{1,0:T(8,128)(2,1)S(1)}, f32[4096,1024]{1,0:T(8,128)S(1)}, bf16[1024,2048]{1,0:T(8,128)(2,1)S(1)}, f32[2560,2048]{1,0:T(8,128)S(1)}, f32[24,128]{1,0:T(8,128)S(1)}) custom-call(bf16[4096,2048]{1,0:T(8,128)(2,1)} %refs_3_.5, s32[1,64]{1,0:T(1,128)} %bitcast.4, s32[1]{0:T(128)S(6)} %copy.69.offset_ref), custom_call_target="tpu_custom_call" | custom-call | bytes 8388608 | tf_op jit(solution)/shard_map/hold_weight/pallas_call | solution.py:120
  7.9 0.3 collective-permute-done.1.refs_1_.refs_2_
  8.2 0.3 collective-permute-start.3
  8.5 0.0 collective-permute-done.refs_0_.refs_1_
  8.5 0.0 copy-start
  8.5 1.9 %collective-permute-start.2 = (bf16[128,2048]{1,0:T(8,128)(2,1)S(1)}, bf16[128,2048]{1,0:T(8,128)(2,1)S(1)}, u32[]{:S(2)}, u32[]{:S(2)}) collective-permute-start(bf16[128,2048]{1,0:T(8,128)(2,1)S(1)} %get-tuple-element.60), channel_id=1, source_target_pairs={{0,8},{2,6},{8,16},{10,2},{16,24},{18,10},{24,28},{26,18},{28,20},... | collective-permute-start | bytes 1572872 | tf_op jit(solution)/shard_map/ppermute | solution.py:462
  10.4 0.0 collective-permute-done.3.refs_3_
  10.4 0.0 copy-done
  10.4 6.3 %score_0.1 = (f32[24,128]{1,0:T(8,128)S(1)}, bf16[4096,2048]{1,0:T(8,128)(2,1)S(1)}, f32[4096,1024]{1,0:T(8,128)S(1)}, bf16[1024,2048]{1,0:T(8,128)(2,1)S(1)}, f32[2560,2048]{1,0:T(8,128)S(1)}) custom-call(bf16[64,2048]{1,0:T(8,128)(2,1)S(1)} %copy-done, ...), custom_call_target="tpu_custom_call", output_to_operand_aliasing={{1}: (7, {}), {2}: (8, {}), {3}: (9, {}), {4}: (10, {})} | custom-call | flops 4294967296 | bytes 17825792 | tf_op jit(solution)/shard_map/score_0/pallas_call | solution.py:219
  16.7 1.0 %collective-permute-done.2.refs_0_ = bf16[128,2048]{1,0:T(8,128)(2,1)S(1)} collective-permute-done((bf16[128,2048]{1,0:T(8,128)(2,1)S(1)}, bf16[128,2048]{1,0:T(8,128)(2,1)S(1)}, u32[]{:S(2)}, u32[]{:S(2)}) %collective-permute-start.2) | collective-permute-done | bytes 524320 | tf_op jit(solution)/shard_map/ppermute | solution.py:462
  17.7 0.0 collective-permute-start.5
  17.7 1.8 %collective-permute-start.4 = (bf16[128,2048]{1,0:T(8,128)(2,1)S(1)}, bf16[128,2048]{1,0:T(8,128)(2,1)S(1)}, u32[]{:S(2)}, u32[]{:S(2)}) collective-permute-start(bf16[128,2048]{1,0:T(8,128)(2,1)S(1)} %collective-permute-done.2.refs_0_), channel_id=1, source_target_pairs={{0,8},{2,6},{8,16},{10,2},{16,24},{18,10},{24,28},{26,18},{28,20},... | collective-permute-start | bytes 1572872 | tf_op jit(solution)/shard_map/ppermute | solution.py:462
  19.6 0.1 collective-permute-done.5.refs_1_
  19.7 5.1 %score_1.1 = (f32[24,128]{1,0:T(8,128)S(1)}, bf16[4096,2048]{1,0:T(8,128)(2,1)S(1)}, f32[4096,1024]{1,0:T(8,128)S(1)}, bf16[1024,2048]{1,0:T(8,128)(2,1)S(1)}, f32[2560,2048]{1,0:T(8,128)S(1)}) custom-call(bf16[128,2048]{1,0:T(8,128)(2,1)S(1)} %collective-permute-done.2.refs_0_, ...), custom_call_target="tpu_custom_call", output_to_operand_aliasing={{1}: (5, {}), {2}: (6, {}), {3}: (7, {}), {4}: (8, {})} | custom-call | flops 4294967296 | bytes 17825792 | tf_op jit(solution)/shard_map/score_1/pallas_call | solution.py:219
  24.8 2.1 %collective-permute-done.4.refs_0_ = bf16[128,2048]{1,0:T(8,128)(2,1)S(1)} collective-permute-done((bf16[128,2048]{1,0:T(8,128)(2,1)S(1)}, bf16[128,2048]{1,0:T(8,128)(2,1)S(1)}, u32[]{:S(2)}, u32[]{:S(2)}) %collective-permute-start.4) | collective-permute-done | bytes 524320 | tf_op jit(solution)/shard_map/ppermute | solution.py:462
  26.9 0.0 collective-permute-start.7
  26.9 1.8 %collective-permute-start.6 = (bf16[128,2048]{1,0:T(8,128)(2,1)S(1)}, bf16[128,2048]{1,0:T(8,128)(2,1)S(1)}, u32[]{:S(2)}, u32[]{:S(2)}) collective-permute-start(bf16[128,2048]{1,0:T(8,128)(2,1)S(1)} %collective-permute-done.4.refs_0_), channel_id=1, source_target_pairs={{0,8},{2,6},{8,16},{10,2},{16,24},{18,10},{24,28},{26,18},{28,20},... | collective-permute-start | bytes 1572872 | tf_op jit(solution)/shard_map/ppermute | solution.py:462
  28.8 0.1 collective-permute-done.7.refs_1_
  28.8 5.1 %score_2.1 = (f32[24,128]{1,0:T(8,128)S(1)}, bf16[4096,2048]{1,0:T(8,128)(2,1)S(1)}, f32[4096,1024]{1,0:T(8,128)S(1)}, bf16[1024,2048]{1,0:T(8,128)(2,1)S(1)}, f32[2560,2048]{1,0:T(8,128)S(1)}) custom-call(bf16[128,2048]{1,0:T(8,128)(2,1)S(1)} %collective-permute-done.4.refs_0_, ...), custom_call_target="tpu_custom_call", output_to_operand_aliasing={{1}: (5, {}), {2}: (6, {}), {3}: (7, {}), {4}: (8, {})} | custom-call | flops 4294967296 | bytes 17825792 | tf_op jit(solution)/shard_map/score_2/pallas_call | solution.py:219
  34.0 2.2 %collective-permute-done.6.refs_0_ = bf16[128,2048]{1,0:T(8,128)(2,1)S(1)} collective-permute-done((bf16[128,2048]{1,0:T(8,128)(2,1)S(1)}, bf16[128,2048]{1,0:T(8,128)(2,1)S(1)}, u32[]{:S(2)}, u32[]{:S(2)}) %collective-permute-start.6) | collective-permute-done | bytes 524320 | tf_op jit(solution)/shard_map/ppermute | solution.py:462
  36.1 0.0 collective-permute-start.8
  36.1 1.9 %collective-permute-done.8.refs_1_ = bf16[128,2048]{1,0:T(8,128)(2,1)S(1)} collective-permute-done((bf16[128,2048]{1,0:T(8,128)(2,1)S(1)}, bf16[128,2048]{1,0:T(8,128)(2,1)S(1)}, u32[]{:S(2)}, u32[]{:S(2)}) %collective-permute-start.8) | collective-permute-done | bytes 524320 | tf_op jit(solution)/shard_map/ppermute | solution.py:459
  38.0 5.1 %score_3.1 = (f32[24,128]{1,0:T(8,128)S(1)}, bf16[4096,2048]{1,0:T(8,128)(2,1)S(1)}, f32[4096,1024]{1,0:T(8,128)S(1)}, bf16[1024,2048]{1,0:T(8,128)(2,1)S(1)}, f32[2560,2048]{1,0:T(8,128)S(1)}) custom-call(bf16[128,2048]{1,0:T(8,128)(2,1)S(1)} %collective-permute-done.6.refs_0_, ...), custom_call_target="tpu_custom_call", output_to_operand_aliasing={{1}: (5, {}), {2}: (6, {}), {3}: (7, {}), {4}: (8, {})} | custom-call | flops 4294967296 | bytes 17825792 | tf_op jit(solution)/shard_map/score_3/pallas_call | solution.py:219
  43.1 0.2 collective-permute-start.9
  43.4 1.0 %collective-permute-done.9.refs_1_ = f32[24,128]{1,0:T(8,128)S(1)} collective-permute-done((f32[24,128]{1,0:T(8,128)S(1)}, f32[24,128]{1,0:T(8,128)S(1)}, u32[]{:S(2)}, u32[]{:S(2)}) %collective-permute-start.9) | collective-permute-done | bytes 12320 | tf_op jit(solution)/shard_map/ppermute | solution.py:444
  44.4 2.8 %collective-permute-start.12 = (f32[24,128]{1,0:T(8,128)S(1)}, f32[24,128]{1,0:T(8,128)S(1)}, u32[]{:S(2)}, u32[]{:S(2)}) collective-permute-start(f32[24,128]{1,0:T(8,128)S(1)} %get-tuple-element.92.refs_0_), channel_id=1, source_target_pairs={{0,5},{1,4},{2,7},{3,6},{4,1},{5,0},{6,3},{7,2},{8,13},{9,12},{10,... | collective-permute-start | bytes 36872 | tf_op jit(solution)/shard_map/ppermute | solution.py:444
  47.2 0.5 collective-permute-start.11
  47.7 0.3 collective-permute-start.10
  47.9 1.1 %collective-permute-done.12.refs_3_ = f32[24,128]{1,0:T(8,128)S(1)} collective-permute-done((f32[24,128]{1,0:T(8,128)S(1)}, f32[24,128]{1,0:T(8,128)S(1)}, u32[]{:S(2)}, u32[]{:S(2)}) %collective-permute-start.12) | collective-permute-done | bytes 12320 | tf_op jit(solution)/shard_map/ppermute | solution.py:444
  49.1 1.8 %collective-permute-done.11.refs_2_ = f32[24,128]{1,0:T(8,128)S(1)} collective-permute-done((f32[24,128]{1,0:T(8,128)S(1)}, f32[24,128]{1,0:T(8,128)S(1)}, u32[]{:S(2)}, u32[]{:S(2)}) %collective-permute-start.11) | collective-permute-done | bytes 12320 | tf_op jit(solution)/shard_map/ppermute | solution.py:444
  50.9 0.5 collective-permute-done.10.refs_1_
  51.4 3.7 %collective-permute-start.15 = (f32[24,128]{1,0:T(8,128)S(1)}, f32[24,128]{1,0:T(8,128)S(1)}, u32[]{:S(2)}, u32[]{:S(2)}) collective-permute-start(f32[24,128]{1,0:T(8,128)S(1)} %get-tuple-element.97.refs_0_), channel_id=1, source_target_pairs={{0,24},{1,25},{2,26},{3,27},{4,28},{5,29},{6,30},{7,31},{8,16},{9,... | collective-permute-start | bytes 36872 | tf_op jit(solution)/shard_map/ppermute | solution.py:444
  55.1 0.0 collective-permute-start.14
  55.1 0.8 collective-permute-start.13
  55.8 1.1 %collective-permute-done.15.refs_3_ = f32[24,128]{1,0:T(8,128)S(1)} collective-permute-done((f32[24,128]{1,0:T(8,128)S(1)}, f32[24,128]{1,0:T(8,128)S(1)}, u32[]{:S(2)}, u32[]{:S(2)}) %collective-permute-start.15) | collective-permute-done | bytes 12320 | tf_op jit(solution)/shard_map/ppermute | solution.py:444
  57.0 2.7 %collective-permute-done.14.refs_2_ = f32[24,128]{1,0:T(8,128)S(1)} collective-permute-done((f32[24,128]{1,0:T(8,128)S(1)}, f32[24,128]{1,0:T(8,128)S(1)}, u32[]{:S(2)}, u32[]{:S(2)}) %collective-permute-start.14) | collective-permute-done | bytes 12320 | tf_op jit(solution)/shard_map/ppermute | solution.py:444
  59.7 0.0 collective-permute-done.13.refs_1_
  59.7 30.0 %update.1 = (bf16[4096,2048]{1,0:T(8,128)(2,1)S(1)}, f32[2560,2048]{1,0:T(8,128)S(1)}, bf16[4096,2048]{1,0:T(8,128)(2,1)}, f32[4096,2048]{1,0:T(8,128)}, f32[1,64]{1,0:T(1,128)}) custom-call(f32[24,128]{1,0:T(8,128)S(1)} %get-tuple-element.97.refs_0_, f32[24,128]{1,0:T(8,128)S(1)} %collective-permute-done.13.refs_1_, ...), custom_call_target="tpu_custom_call", output_to_operand_aliasing={{0}: (8, {}), {1}: (9, {})} | custom-call | flops 17179869184 | bytes 83886080 | tf_op jit(solution)/shard_map/update/pallas_call | solution.py:395
  (3 shorter events, 0.1 us)
Async XLA Ops:
  0.6 7.6 %collective-permute-start.1 = (bf16[64,2048]{1,0:T(8,128)(2,1)}, bf16[64,2048]{1,0:T(8,128)(2,1)S(1)}, u32[]{:S(2)}, u32[]{:S(2)}) collective-permute-start(bf16[64,2048]{1,0:T(8,128)(2,1)} %refs_0_.1), channel_id=1, source_target_pairs={{0,8},{2,6},{8,16},{10,2},{16,24},{18,10},{24,28},{26,18},{28,20},... | collective-permute-start | bytes 786440 | tf_op jit(solution)/shard_map/ppermute | solution.py:462
  3.7 4.8 %collective-permute-start = (bf16[64,2048]{1,0:T(8,128)(2,1)}, bf16[64,2048]{1,0:T(8,128)(2,1)S(1)}, u32[]{:S(2)}, u32[]{:S(2)}) collective-permute-start(bf16[64,2048]{1,0:T(8,128)(2,1)} %refs_0_.1), channel_id=1, source_target_pairs={{0,2},{2,0},{4,6},{6,4},{8,10},{10,8},{12,14},{14,12},{16,18},{18,... | collective-permute-start | bytes 786440 | tf_op jit(solution)/shard_map/ppermute | solution.py:459
  8.2 2.2 %collective-permute-start.3 = (bf16[64,2048]{1,0:T(8,128)(2,1)S(1)}, bf16[64,2048]{1,0:T(8,128)(2,1)S(1)}, u32[]{:S(2)}, u32[]{:S(2)}) collective-permute-start(bf16[64,2048]{1,0:T(8,128)(2,1)S(1)} %collective-permute-done.1.refs_1_.refs_2_), channel_id=1, source_target_pairs={{0,2},{2,0},{4,6},{6,4},{8,10},{10,8},{12,14},{14,12},{16,18},{18,... | collective-permute-start | bytes 786440 | tf_op jit(solution)/shard_map/ppermute | solution.py:459
  8.5 1.9 %copy-start = (bf16[64,2048]{1,0:T(8,128)(2,1)S(1)}, bf16[64,2048]{1,0:T(8,128)(2,1)}, u32[]{:S(2)}) copy-start(bf16[64,2048]{1,0:T(8,128)(2,1)} %refs_0_.1) | copy-start | bytes 786436
  8.5 9.2 %collective-permute-start.2 = (bf16[128,2048]{1,0:T(8,128)(2,1)S(1)}, bf16[128,2048]{1,0:T(8,128)(2,1)S(1)}, u32[]{:S(2)}, u32[]{:S(2)}) collective-permute-start(bf16[128,2048]{1,0:T(8,128)(2,1)S(1)} %get-tuple-element.60), channel_id=1, source_target_pairs={{0,8},{2,6},{8,16},{10,2},{16,24},{18,10},{24,28},{26,18},{28,20},... | collective-permute-start | bytes 1572872 | tf_op jit(solution)/shard_map/ppermute | solution.py:462
  17.7 1.9 %collective-permute-start.5 = (bf16[128,2048]{1,0:T(8,128)(2,1)S(1)}, bf16[128,2048]{1,0:T(8,128)(2,1)S(1)}, u32[]{:S(2)}, u32[]{:S(2)}) collective-permute-start(bf16[128,2048]{1,0:T(8,128)(2,1)S(1)} %collective-permute-done.2.refs_0_), channel_id=1, source_target_pairs={{0,2},{2,0},{4,6},{6,4},{8,10},{10,8},{12,14},{14,12},{16,18},{18,... | collective-permute-start | bytes 1572872 | tf_op jit(solution)/shard_map/ppermute | solution.py:459
  17.7 9.2 %collective-permute-start.4 = (bf16[128,2048]{1,0:T(8,128)(2,1)S(1)}, bf16[128,2048]{1,0:T(8,128)(2,1)S(1)}, u32[]{:S(2)}, u32[]{:S(2)}) collective-permute-start(bf16[128,2048]{1,0:T(8,128)(2,1)S(1)} %collective-permute-done.2.refs_0_), channel_id=1, source_target_pairs={{0,8},{2,6},{8,16},{10,2},{16,24},{18,10},{24,28},{26,18},{28,20},... | collective-permute-start | bytes 1572872 | tf_op jit(solution)/shard_map/ppermute | solution.py:462
  26.9 1.9 %collective-permute-start.7 = (bf16[128,2048]{1,0:T(8,128)(2,1)S(1)}, bf16[128,2048]{1,0:T(8,128)(2,1)S(1)}, u32[]{:S(2)}, u32[]{:S(2)}) collective-permute-start(bf16[128,2048]{1,0:T(8,128)(2,1)S(1)} %collective-permute-done.4.refs_0_), channel_id=1, source_target_pairs={{0,2},{2,0},{4,6},{6,4},{8,10},{10,8},{12,14},{14,12},{16,18},{18,... | collective-permute-start | bytes 1572872 | tf_op jit(solution)/shard_map/ppermute | solution.py:459
  26.9 9.2 %collective-permute-start.6 = (bf16[128,2048]{1,0:T(8,128)(2,1)S(1)}, bf16[128,2048]{1,0:T(8,128)(2,1)S(1)}, u32[]{:S(2)}, u32[]{:S(2)}) collective-permute-start(bf16[128,2048]{1,0:T(8,128)(2,1)S(1)} %collective-permute-done.4.refs_0_), channel_id=1, source_target_pairs={{0,8},{2,6},{8,16},{10,2},{16,24},{18,10},{24,28},{26,18},{28,20},... | collective-permute-start | bytes 1572872 | tf_op jit(solution)/shard_map/ppermute | solution.py:462
  36.1 1.9 %collective-permute-start.8 = (bf16[128,2048]{1,0:T(8,128)(2,1)S(1)}, bf16[128,2048]{1,0:T(8,128)(2,1)S(1)}, u32[]{:S(2)}, u32[]{:S(2)}) collective-permute-start(bf16[128,2048]{1,0:T(8,128)(2,1)S(1)} %collective-permute-done.6.refs_0_), channel_id=1, source_target_pairs={{0,2},{2,0},{4,6},{6,4},{8,10},{10,8},{12,14},{14,12},{16,18},{18,... | collective-permute-start | bytes 1572872 | tf_op jit(solution)/shard_map/ppermute | solution.py:459
  43.1 1.2 %collective-permute-start.9 = (f32[24,128]{1,0:T(8,128)S(1)}, f32[24,128]{1,0:T(8,128)S(1)}, u32[]{:S(2)}, u32[]{:S(2)}) collective-permute-start(f32[24,128]{1,0:T(8,128)S(1)} %get-tuple-element.87.refs_0_), channel_id=1, source_target_pairs={{0,2},{1,3},{2,0},{3,1},{4,6},{5,7},{6,4},{7,5},{8,10},{9,11},{10,... | collective-permute-start | bytes 36872 | tf_op jit(solution)/shard_map/ppermute | solution.py:444
  44.4 4.7 %collective-permute-start.12 = (f32[24,128]{1,0:T(8,128)S(1)}, f32[24,128]{1,0:T(8,128)S(1)}, u32[]{:S(2)}, u32[]{:S(2)}) collective-permute-start(f32[24,128]{1,0:T(8,128)S(1)} %get-tuple-element.92.refs_0_), channel_id=1, source_target_pairs={{0,5},{1,4},{2,7},{3,6},{4,1},{5,0},{6,3},{7,2},{8,13},{9,12},{10,... | collective-permute-start | bytes 36872 | tf_op jit(solution)/shard_map/ppermute | solution.py:444
  47.2 3.7 %collective-permute-start.11 = (f32[24,128]{1,0:T(8,128)S(1)}, f32[24,128]{1,0:T(8,128)S(1)}, u32[]{:S(2)}, u32[]{:S(2)}) collective-permute-start(f32[24,128]{1,0:T(8,128)S(1)} %get-tuple-element.92.refs_0_), channel_id=1, source_target_pairs={{0,4},{1,5},{2,6},{3,7},{4,0},{5,1},{6,2},{7,3},{8,12},{9,13},{10,... | collective-permute-start | bytes 36872 | tf_op jit(solution)/shard_map/ppermute | solution.py:444
  47.7 3.7 %collective-permute-start.10 = (f32[24,128]{1,0:T(8,128)S(1)}, f32[24,128]{1,0:T(8,128)S(1)}, u32[]{:S(2)}, u32[]{:S(2)}) collective-permute-start(f32[24,128]{1,0:T(8,128)S(1)} %get-tuple-element.92.refs_0_), channel_id=1, source_target_pairs={{0,1},{1,0},{2,3},{3,2},{4,5},{5,4},{6,7},{7,6},{8,9},{9,8},{10,11... | collective-permute-start | bytes 36872 | tf_op jit(solution)/shard_map/ppermute | solution.py:444
  51.4 5.6 %collective-permute-start.15 = (f32[24,128]{1,0:T(8,128)S(1)}, f32[24,128]{1,0:T(8,128)S(1)}, u32[]{:S(2)}, u32[]{:S(2)}) collective-permute-start(f32[24,128]{1,0:T(8,128)S(1)} %get-tuple-element.97.refs_0_), channel_id=1, source_target_pairs={{0,24},{1,25},{2,26},{3,27},{4,28},{5,29},{6,30},{7,31},{8,16},{9,... | collective-permute-start | bytes 36872 | tf_op jit(solution)/shard_map/ppermute | solution.py:444
  55.1 4.6 %collective-permute-start.14 = (f32[24,128]{1,0:T(8,128)S(1)}, f32[24,128]{1,0:T(8,128)S(1)}, u32[]{:S(2)}, u32[]{:S(2)}) collective-permute-start(f32[24,128]{1,0:T(8,128)S(1)} %get-tuple-element.97.refs_0_), channel_id=1, source_target_pairs={{0,16},{1,17},{2,18},{3,19},{4,20},{5,21},{6,22},{7,23},{8,24},{9,... | collective-permute-start | bytes 36872 | tf_op jit(solution)/shard_map/ppermute | solution.py:444
  55.1 4.6 %collective-permute-start.13 = (f32[24,128]{1,0:T(8,128)S(1)}, f32[24,128]{1,0:T(8,128)S(1)}, u32[]{:S(2)}, u32[]{:S(2)}) collective-permute-start(f32[24,128]{1,0:T(8,128)S(1)} %get-tuple-element.97.refs_0_), channel_id=1, source_target_pairs={{0,8},{1,9},{2,10},{3,11},{4,12},{5,13},{6,14},{7,15},{8,0},{9,1},... | collective-permute-start | bytes 36872 | tf_op jit(solution)/shard_map/ppermute | solution.py:444

commit v4 on v3

--- a/solution.py
+++ b/solution.py
@@ -344,17 +344,18 @@
                 delta_s[now], x_ref[:, pl.ds(n * bn, bn)], preferred_element_type=f32
             )
 
+        acc_rows, w_rows = acc_ref.at[rows_of(slot)], w_ref.at[rows_of(i)]
+
         def update_tile(n):
             cols = pl.ds(n * bn, bn)
             for r in range(0, bm, SUB):
-                a_rows = pl.ds(pl.multiple_of(slot * bm + r, SUB), SUB)
-                w_rows = pl.ds(pl.multiple_of(i * bm + r, SUB), SUB)
-                grad = grad_s[n % 2, pl.ds(r, SUB), :]
-                new_acc = acc_ref[a_rows, cols] + grad * grad
-                acc_ref[a_rows, cols] = new_acc
+                here = pl.ds(r, SUB)
+                grad = grad_s[n % 2, here, :]
+                new_acc = acc_rows[here, cols] + grad * grad
+                acc_rows[here, cols] = new_acc
                 root = new_acc * lax.rsqrt(new_acc)
                 part = (0.05 * grad) * pltpu.reciprocal(root + 1e-10, approx=True)
-                w_ref[w_rows, cols] = (w_ref[w_rows, cols].astype(f32) - part).astype(bf16)
+                w_rows[here, cols] = (w_rows[here, cols].astype(f32) - part).astype(bf16)
 
         tiles = feats // bn
         grad_tile(0)

time: 90 us -> 88.5 us (0.983)
  Pallas kernels: 55.2 us -> 53.7 us
    pallas_call x1, Pallas kernels: 30 us -> 28.5 us  [update(): pl.pallas_call(functools.partial(update_kernel, cfg), name='update', out_...]
  transfers between devices with their start and end apart: 16 -> 16, of which waited for: 13 -> 13; matrix products, arithmetic and copies ran while one was open for 0% -> 0% of each run, Pallas kernels for 22% -> 23%
where the time goes in v4:
time: 88.5 us; the launch traced here: 88.3 us
  Pallas kernels  53.7 us (61%)
  starting transfers between devices  17.1 us (19%)
  waiting for transfers between devices  16 us (18%)
  between operations  1.51 us (2%)
    pallas_call x1, Pallas kernels, update(): pl.pallas_call(functools.partial(update_kernel, cfg), name='update', out_...  28.5 us
    pallas_call x4, Pallas kernels, score(): pl.pallas_call(functools.partial(score_kernel, cfg), name=f'score_{k}', o...  21.6 us
    ppermute x4, starting transfers between devices, round_ring(): return lax.ppermute(x, 'blk', ring_pairs(chips))  8.64 us
    ppermute x7, waiting for transfers between devices, exchange_stats(): messages.append(lax.ppermute(message, ('blk', 'cls'), pairs))  8.27 us
    ppermute x7, starting transfers between devices, exchange_stats(): messages.append(lax.ppermute(message, ('blk', 'cls'), pairs))  8.2 us
    ppermute x4, waiting for transfers between devices, round_ring(): return lax.ppermute(x, 'blk', ring_pairs(chips))  5.66 us
    pallas_call x1, Pallas kernels, hold(): pl.pallas_call(functools.partial(hold_kernel, chips), name='hold_weight',...  3.51 us
    ppermute x5, waiting for transfers between devices, swap_cores(): return lax.ppermute(x, 'blk', [(d, d ^ 1) for d in range(blk_size)])  2.05 us
  transfers between devices with their start and end apart: 16, of which 13 were waited for; matrix products, arithmetic and copies ran while one was open for 0% of the time, Pallas kernels for 23%

profile of v4, /device:TPU:0, one launch (start us, length us, event | category | flops | bytes accessed | tf_op | source)
XLA Modules:
  0.0 88.3 jit_solution(13847320125400468952)
XLA Ops:
  0.6 3.1 %collective-permute-start.1 = (bf16[64,2048]{1,0:T(8,128)(2,1)}, bf16[64,2048]{1,0:T(8,128)(2,1)S(1)}, u32[]{:S(2)}, u32[]{:S(2)}) collective-permute-start(bf16[64,2048]{1,0:T(8,128)(2,1)} %refs_0_.1), channel_id=1, source_target_pairs={{0,8},{2,6},{8,16},{10,2},{16,24},{18,10},{24,28},{26,18},{28,20},... | collective-permute-start | bytes 786440 | tf_op jit(solution)/shard_map/ppermute | solution.py:463
  3.7 0.0 collective-permute-start
  4.4 3.5 %hold_weight.1 = (bf16[4096,2048]{1,0:T(8,128)(2,1)S(1)}, f32[4096,1024]{1,0:T(8,128)S(1)}, bf16[1024,2048]{1,0:T(8,128)(2,1)S(1)}, f32[2560,2048]{1,0:T(8,128)S(1)}, f32[24,128]{1,0:T(8,128)S(1)}) custom-call(bf16[4096,2048]{1,0:T(8,128)(2,1)} %refs_3_.5, s32[1,64]{1,0:T(1,128)} %bitcast.4, s32[1]{0:T(128)S(6)} %copy.69.offset_ref), custom_call_target="tpu_custom_call" | custom-call | bytes 8388608 | tf_op jit(solution)/shard_map/hold_weight/pallas_call | solution.py:120
  7.9 0.3 collective-permute-done.1.refs_1_.refs_2_
  8.2 0.3 collective-permute-start.3
  8.5 0.0 collective-permute-done.refs_0_.refs_1_
  8.5 0.0 copy-start
  8.5 1.9 %collective-permute-start.2 = (bf16[128,2048]{1,0:T(8,128)(2,1)S(1)}, bf16[128,2048]{1,0:T(8,128)(2,1)S(1)}, u32[]{:S(2)}, u32[]{:S(2)}) collective-permute-start(bf16[128,2048]{1,0:T(8,128)(2,1)S(1)} %get-tuple-element.60), channel_id=1, source_target_pairs={{0,8},{2,6},{8,16},{10,2},{16,24},{18,10},{24,28},{26,18},{28,20},... | collective-permute-start | bytes 1572872 | tf_op jit(solution)/shard_map/ppermute | solution.py:463
  10.4 0.0 collective-permute-done.3.refs_3_
  10.4 0.0 copy-done
  10.4 6.3 %score_0.1 = (f32[24,128]{1,0:T(8,128)S(1)}, bf16[4096,2048]{1,0:T(8,128)(2,1)S(1)}, f32[4096,1024]{1,0:T(8,128)S(1)}, bf16[1024,2048]{1,0:T(8,128)(2,1)S(1)}, f32[2560,2048]{1,0:T(8,128)S(1)}) custom-call(bf16[64,2048]{1,0:T(8,128)(2,1)S(1)} %copy-done, ...), custom_call_target="tpu_custom_call", output_to_operand_aliasing={{1}: (7, {}), {2}: (8, {}), {3}: (9, {}), {4}: (10, {})} | custom-call | flops 4294967296 | bytes 17825792 | tf_op jit(solution)/shard_map/score_0/pallas_call | solution.py:219
  16.7 1.0 %collective-permute-done.2.refs_0_ = bf16[128,2048]{1,0:T(8,128)(2,1)S(1)} collective-permute-done((bf16[128,2048]{1,0:T(8,128)(2,1)S(1)}, bf16[128,2048]{1,0:T(8,128)(2,1)S(1)}, u32[]{:S(2)}, u32[]{:S(2)}) %collective-permute-start.2) | collective-permute-done | bytes 524320 | tf_op jit(solution)/shard_map/ppermute | solution.py:463
  17.7 0.0 collective-permute-start.5
  17.7 1.8 %collective-permute-start.4 = (bf16[128,2048]{1,0:T(8,128)(2,1)S(1)}, bf16[128,2048]{1,0:T(8,128)(2,1)S(1)}, u32[]{:S(2)}, u32[]{:S(2)}) collective-permute-start(bf16[128,2048]{1,0:T(8,128)(2,1)S(1)} %collective-permute-done.2.refs_0_), channel_id=1, source_target_pairs={{0,8},{2,6},{8,16},{10,2},{16,24},{18,10},{24,28},{26,18},{28,20},... | collective-permute-start | bytes 1572872 | tf_op jit(solution)/shard_map/ppermute | solution.py:463
  19.6 0.1 collective-permute-done.5.refs_1_
  19.7 5.1 %score_1.1 = (f32[24,128]{1,0:T(8,128)S(1)}, bf16[4096,2048]{1,0:T(8,128)(2,1)S(1)}, f32[4096,1024]{1,0:T(8,128)S(1)}, bf16[1024,2048]{1,0:T(8,128)(2,1)S(1)}, f32[2560,2048]{1,0:T(8,128)S(1)}) custom-call(bf16[128,2048]{1,0:T(8,128)(2,1)S(1)} %collective-permute-done.2.refs_0_, ...), custom_call_target="tpu_custom_call", output_to_operand_aliasing={{1}: (5, {}), {2}: (6, {}), {3}: (7, {}), {4}: (8, {})} | custom-call | flops 4294967296 | bytes 17825792 | tf_op jit(solution)/shard_map/score_1/pallas_call | solution.py:219
  24.8 2.1 %collective-permute-done.4.refs_0_ = bf16[128,2048]{1,0:T(8,128)(2,1)S(1)} collective-permute-done((bf16[128,2048]{1,0:T(8,128)(2,1)S(1)}, bf16[128,2048]{1,0:T(8,128)(2,1)S(1)}, u32[]{:S(2)}, u32[]{:S(2)}) %collective-permute-start.4) | collective-permute-done | bytes 524320 | tf_op jit(solution)/shard_map/ppermute | solution.py:463
  26.9 0.0 collective-permute-start.7
  26.9 1.8 %collective-permute-start.6 = (bf16[128,2048]{1,0:T(8,128)(2,1)S(1)}, bf16[128,2048]{1,0:T(8,128)(2,1)S(1)}, u32[]{:S(2)}, u32[]{:S(2)}) collective-permute-start(bf16[128,2048]{1,0:T(8,128)(2,1)S(1)} %collective-permute-done.4.refs_0_), channel_id=1, source_target_pairs={{0,8},{2,6},{8,16},{10,2},{16,24},{18,10},{24,28},{26,18},{28,20},... | collective-permute-start | bytes 1572872 | tf_op jit(solution)/shard_map/ppermute | solution.py:463
  28.8 0.1 collective-permute-done.7.refs_1_
  28.8 5.1 %score_2.1 = (f32[24,128]{1,0:T(8,128)S(1)}, bf16[4096,2048]{1,0:T(8,128)(2,1)S(1)}, f32[4096,1024]{1,0:T(8,128)S(1)}, bf16[1024,2048]{1,0:T(8,128)(2,1)S(1)}, f32[2560,2048]{1,0:T(8,128)S(1)}) custom-call(bf16[128,2048]{1,0:T(8,128)(2,1)S(1)} %collective-permute-done.4.refs_0_, ...), custom_call_target="tpu_custom_call", output_to_operand_aliasing={{1}: (5, {}), {2}: (6, {}), {3}: (7, {}), {4}: (8, {})} | custom-call | flops 4294967296 | bytes 17825792 | tf_op jit(solution)/shard_map/score_2/pallas_call | solution.py:219
  34.0 2.2 %collective-permute-done.6.refs_0_ = bf16[128,2048]{1,0:T(8,128)(2,1)S(1)} collective-permute-done((bf16[128,2048]{1,0:T(8,128)(2,1)S(1)}, bf16[128,2048]{1,0:T(8,128)(2,1)S(1)}, u32[]{:S(2)}, u32[]{:S(2)}) %collective-permute-start.6) | collective-permute-done | bytes 524320 | tf_op jit(solution)/shard_map/ppermute | solution.py:463
  36.1 0.0 collective-permute-start.8
  36.1 1.9 %collective-permute-done.8.refs_1_ = bf16[128,2048]{1,0:T(8,128)(2,1)S(1)} collective-permute-done((bf16[128,2048]{1,0:T(8,128)(2,1)S(1)}, bf16[128,2048]{1,0:T(8,128)(2,1)S(1)}, u32[]{:S(2)}, u32[]{:S(2)}) %collective-permute-start.8) | collective-permute-done | bytes 524320 | tf_op jit(solution)/shard_map/ppermute | solution.py:460
  38.0 5.1 %score_3.1 = (f32[24,128]{1,0:T(8,128)S(1)}, bf16[4096,2048]{1,0:T(8,128)(2,1)S(1)}, f32[4096,1024]{1,0:T(8,128)S(1)}, bf16[1024,2048]{1,0:T(8,128)(2,1)S(1)}, f32[2560,2048]{1,0:T(8,128)S(1)}) custom-call(bf16[128,2048]{1,0:T(8,128)(2,1)S(1)} %collective-permute-done.6.refs_0_, ...), custom_call_target="tpu_custom_call", output_to_operand_aliasing={{1}: (5, {}), {2}: (6, {}), {3}: (7, {}), {4}: (8, {})} | custom-call | flops 4294967296 | bytes 17825792 | tf_op jit(solution)/shard_map/score_3/pallas_call | solution.py:219
  43.1 0.2 collective-permute-start.9
  43.4 1.0 %collective-permute-done.9.refs_1_ = f32[24,128]{1,0:T(8,128)S(1)} collective-permute-done((f32[24,128]{1,0:T(8,128)S(1)}, f32[24,128]{1,0:T(8,128)S(1)}, u32[]{:S(2)}, u32[]{:S(2)}) %collective-permute-start.9) | collective-permute-done | bytes 12320 | tf_op jit(solution)/shard_map/ppermute | solution.py:445
  44.4 2.8 %collective-permute-start.12 = (f32[24,128]{1,0:T(8,128)S(1)}, f32[24,128]{1,0:T(8,128)S(1)}, u32[]{:S(2)}, u32[]{:S(2)}) collective-permute-start(f32[24,128]{1,0:T(8,128)S(1)} %get-tuple-element.92.refs_0_), channel_id=1, source_target_pairs={{0,5},{1,4},{2,7},{3,6},{4,1},{5,0},{6,3},{7,2},{8,13},{9,12},{10,... | collective-permute-start | bytes 36872 | tf_op jit(solution)/shard_map/ppermute | solution.py:445
  47.2 0.5 collective-permute-start.11
  47.7 0.3 collective-permute-start.10
  47.9 1.1 %collective-permute-done.12.refs_3_ = f32[24,128]{1,0:T(8,128)S(1)} collective-permute-done((f32[24,128]{1,0:T(8,128)S(1)}, f32[24,128]{1,0:T(8,128)S(1)}, u32[]{:S(2)}, u32[]{:S(2)}) %collective-permute-start.12) | collective-permute-done | bytes 12320 | tf_op jit(solution)/shard_map/ppermute | solution.py:445
  49.1 1.8 %collective-permute-done.11.refs_2_ = f32[24,128]{1,0:T(8,128)S(1)} collective-permute-done((f32[24,128]{1,0:T(8,128)S(1)}, f32[24,128]{1,0:T(8,128)S(1)}, u32[]{:S(2)}, u32[]{:S(2)}) %collective-permute-start.11) | collective-permute-done | bytes 12320 | tf_op jit(solution)/shard_map/ppermute | solution.py:445
  50.9 0.5 collective-permute-done.10.refs_1_
  51.4 3.7 %collective-permute-start.15 = (f32[24,128]{1,0:T(8,128)S(1)}, f32[24,128]{1,0:T(8,128)S(1)}, u32[]{:S(2)}, u32[]{:S(2)}) collective-permute-start(f32[24,128]{1,0:T(8,128)S(1)} %get-tuple-element.97.refs_0_), channel_id=1, source_target_pairs={{0,24},{1,25},{2,26},{3,27},{4,28},{5,29},{6,30},{7,31},{8,16},{9,... | collective-permute-start | bytes 36872 | tf_op jit(solution)/shard_map/ppermute | solution.py:445
  55.1 0.0 collective-permute-start.14
  55.1 0.8 collective-permute-start.13
  55.8 1.1 %collective-permute-done.15.refs_3_ = f32[24,128]{1,0:T(8,128)S(1)} collective-permute-done((f32[24,128]{1,0:T(8,128)S(1)}, f32[24,128]{1,0:T(8,128)S(1)}, u32[]{:S(2)}, u32[]{:S(2)}) %collective-permute-start.15) | collective-permute-done | bytes 12320 | tf_op jit(solution)/shard_map/ppermute | solution.py:445
  57.0 2.7 %collective-permute-done.14.refs_2_ = f32[24,128]{1,0:T(8,128)S(1)} collective-permute-done((f32[24,128]{1,0:T(8,128)S(1)}, f32[24,128]{1,0:T(8,128)S(1)}, u32[]{:S(2)}, u32[]{:S(2)}) %collective-permute-start.14) | collective-permute-done | bytes 12320 | tf_op jit(solution)/shard_map/ppermute | solution.py:445
  59.7 0.0 collective-permute-done.13.refs_1_
  59.7 28.5 %update.1 = (bf16[4096,2048]{1,0:T(8,128)(2,1)S(1)}, f32[2560,2048]{1,0:T(8,128)S(1)}, bf16[4096,2048]{1,0:T(8,128)(2,1)}, f32[4096,2048]{1,0:T(8,128)}, f32[1,64]{1,0:T(1,128)}) custom-call(f32[24,128]{1,0:T(8,128)S(1)} %get-tuple-element.97.refs_0_, f32[24,128]{1,0:T(8,128)S(1)} %collective-permute-done.13.refs_1_, ...), custom_call_target="tpu_custom_call", output_to_operand_aliasing={{0}: (8, {}), {1}: (9, {})} | custom-call | flops 17179869184 | bytes 83886080 | tf_op jit(solution)/shard_map/update/pallas_call | solution.py:396
  (3 shorter events, 0.1 us)
Async XLA Ops:
  0.6 7.6 %collective-permute-start.1 = (bf16[64,2048]{1,0:T(8,128)(2,1)}, bf16[64,2048]{1,0:T(8,128)(2,1)S(1)}, u32[]{:S(2)}, u32[]{:S(2)}) collective-permute-start(bf16[64,2048]{1,0:T(8,128)(2,1)} %refs_0_.1), channel_id=1, source_target_pairs={{0,8},{2,6},{8,16},{10,2},{16,24},{18,10},{24,28},{26,18},{28,20},... | collective-permute-start | bytes 786440 | tf_op jit(solution)/shard_map/ppermute | solution.py:463
  3.7 4.8 %collective-permute-start = (bf16[64,2048]{1,0:T(8,128)(2,1)}, bf16[64,2048]{1,0:T(8,128)(2,1)S(1)}, u32[]{:S(2)}, u32[]{:S(2)}) collective-permute-start(bf16[64,2048]{1,0:T(8,128)(2,1)} %refs_0_.1), channel_id=1, source_target_pairs={{0,2},{2,0},{4,6},{6,4},{8,10},{10,8},{12,14},{14,12},{16,18},{18,... | collective-permute-start | bytes 786440 | tf_op jit(solution)/shard_map/ppermute | solution.py:460
  8.2 2.2 %collective-permute-start.3 = (bf16[64,2048]{1,0:T(8,128)(2,1)S(1)}, bf16[64,2048]{1,0:T(8,128)(2,1)S(1)}, u32[]{:S(2)}, u32[]{:S(2)}) collective-permute-start(bf16[64,2048]{1,0:T(8,128)(2,1)S(1)} %collective-permute-done.1.refs_1_.refs_2_), channel_id=1, source_target_pairs={{0,2},{2,0},{4,6},{6,4},{8,10},{10,8},{12,14},{14,12},{16,18},{18,... | collective-permute-start | bytes 786440 | tf_op jit(solution)/shard_map/ppermute | solution.py:460
  8.5 1.9 %copy-start = (bf16[64,2048]{1,0:T(8,128)(2,1)S(1)}, bf16[64,2048]{1,0:T(8,128)(2,1)}, u32[]{:S(2)}) copy-start(bf16[64,2048]{1,0:T(8,128)(2,1)} %refs_0_.1) | copy-start | bytes 786436
  8.5 9.2 %collective-permute-start.2 = (bf16[128,2048]{1,0:T(8,128)(2,1)S(1)}, bf16[128,2048]{1,0:T(8,128)(2,1)S(1)}, u32[]{:S(2)}, u32[]{:S(2)}) collective-permute-start(bf16[128,2048]{1,0:T(8,128)(2,1)S(1)} %get-tuple-element.60), channel_id=1, source_target_pairs={{0,8},{2,6},{8,16},{10,2},{16,24},{18,10},{24,28},{26,18},{28,20},... | collective-permute-start | bytes 1572872 | tf_op jit(solution)/shard_map/ppermute | solution.py:463
  17.7 1.9 %collective-permute-start.5 = (bf16[128,2048]{1,0:T(8,128)(2,1)S(1)}, bf16[128,2048]{1,0:T(8,128)(2,1)S(1)}, u32[]{:S(2)}, u32[]{:S(2)}) collective-permute-start(bf16[128,2048]{1,0:T(8,128)(2,1)S(1)} %collective-permute-done.2.refs_0_), channel_id=1, source_target_pairs={{0,2},{2,0},{4,6},{6,4},{8,10},{10,8},{12,14},{14,12},{16,18},{18,... | collective-permute-start | bytes 1572872 | tf_op jit(solution)/shard_map/ppermute | solution.py:460
  17.7 9.2 %collective-permute-start.4 = (bf16[128,2048]{1,0:T(8,128)(2,1)S(1)}, bf16[128,2048]{1,0:T(8,128)(2,1)S(1)}, u32[]{:S(2)}, u32[]{:S(2)}) collective-permute-start(bf16[128,2048]{1,0:T(8,128)(2,1)S(1)} %collective-permute-done.2.refs_0_), channel_id=1, source_target_pairs={{0,8},{2,6},{8,16},{10,2},{16,24},{18,10},{24,28},{26,18},{28,20},... | collective-permute-start | bytes 1572872 | tf_op jit(solution)/shard_map/ppermute | solution.py:463
  26.9 1.9 %collective-permute-start.7 = (bf16[128,2048]{1,0:T(8,128)(2,1)S(1)}, bf16[128,2048]{1,0:T(8,128)(2,1)S(1)}, u32[]{:S(2)}, u32[]{:S(2)}) collective-permute-start(bf16[128,2048]{1,0:T(8,128)(2,1)S(1)} %collective-permute-done.4.refs_0_), channel_id=1, source_target_pairs={{0,2},{2,0},{4,6},{6,4},{8,10},{10,8},{12,14},{14,12},{16,18},{18,... | collective-permute-start | bytes 1572872 | tf_op jit(solution)/shard_map/ppermute | solution.py:460
  26.9 9.2 %collective-permute-start.6 = (bf16[128,2048]{1,0:T(8,128)(2,1)S(1)}, bf16[128,2048]{1,0:T(8,128)(2,1)S(1)}, u32[]{:S(2)}, u32[]{:S(2)}) collective-permute-start(bf16[128,2048]{1,0:T(8,128)(2,1)S(1)} %collective-permute-done.4.refs_0_), channel_id=1, source_target_pairs={{0,8},{2,6},{8,16},{10,2},{16,24},{18,10},{24,28},{26,18},{28,20},... | collective-permute-start | bytes 1572872 | tf_op jit(solution)/shard_map/ppermute | solution.py:463
  36.1 1.9 %collective-permute-start.8 = (bf16[128,2048]{1,0:T(8,128)(2,1)S(1)}, bf16[128,2048]{1,0:T(8,128)(2,1)S(1)}, u32[]{:S(2)}, u32[]{:S(2)}) collective-permute-start(bf16[128,2048]{1,0:T(8,128)(2,1)S(1)} %collective-permute-done.6.refs_0_), channel_id=1, source_target_pairs={{0,2},{2,0},{4,6},{6,4},{8,10},{10,8},{12,14},{14,12},{16,18},{18,... | collective-permute-start | bytes 1572872 | tf_op jit(solution)/shard_map/ppermute | solution.py:460
  43.1 1.2 %collective-permute-start.9 = (f32[24,128]{1,0:T(8,128)S(1)}, f32[24,128]{1,0:T(8,128)S(1)}, u32[]{:S(2)}, u32[]{:S(2)}) collective-permute-start(f32[24,128]{1,0:T(8,128)S(1)} %get-tuple-element.87.refs_0_), channel_id=1, source_target_pairs={{0,2},{1,3},{2,0},{3,1},{4,6},{5,7},{6,4},{7,5},{8,10},{9,11},{10,... | collective-permute-start | bytes 36872 | tf_op jit(solution)/shard_map/ppermute | solution.py:445
  44.4 4.7 %collective-permute-start.12 = (f32[24,128]{1,0:T(8,128)S(1)}, f32[24,128]{1,0:T(8,128)S(1)}, u32[]{:S(2)}, u32[]{:S(2)}) collective-permute-start(f32[24,128]{1,0:T(8,128)S(1)} %get-tuple-element.92.refs_0_), channel_id=1, source_target_pairs={{0,5},{1,4},{2,7},{3,6},{4,1},{5,0},{6,3},{7,2},{8,13},{9,12},{10,... | collective-permute-start | bytes 36872 | tf_op jit(solution)/shard_map/ppermute | solution.py:445
  47.2 3.7 %collective-permute-start.11 = (f32[24,128]{1,0:T(8,128)S(1)}, f32[24,128]{1,0:T(8,128)S(1)}, u32[]{:S(2)}, u32[]{:S(2)}) collective-permute-start(f32[24,128]{1,0:T(8,128)S(1)} %get-tuple-element.92.refs_0_), channel_id=1, source_target_pairs={{0,4},{1,5},{2,6},{3,7},{4,0},{5,1},{6,2},{7,3},{8,12},{9,13},{10,... | collective-permute-start | bytes 36872 | tf_op jit(solution)/shard_map/ppermute | solution.py:445
  47.7 3.7 %collective-permute-start.10 = (f32[24,128]{1,0:T(8,128)S(1)}, f32[24,128]{1,0:T(8,128)S(1)}, u32[]{:S(2)}, u32[]{:S(2)}) collective-permute-start(f32[24,128]{1,0:T(8,128)S(1)} %get-tuple-element.92.refs_0_), channel_id=1, source_target_pairs={{0,1},{1,0},{2,3},{3,2},{4,5},{5,4},{6,7},{7,6},{8,9},{9,8},{10,11... | collective-permute-start | bytes 36872 | tf_op jit(solution)/shard_map/ppermute | solution.py:445
  51.4 5.6 %collective-permute-start.15 = (f32[24,128]{1,0:T(8,128)S(1)}, f32[24,128]{1,0:T(8,128)S(1)}, u32[]{:S(2)}, u32[]{:S(2)}) collective-permute-start(f32[24,128]{1,0:T(8,128)S(1)} %get-tuple-element.97.refs_0_), channel_id=1, source_target_pairs={{0,24},{1,25},{2,26},{3,27},{4,28},{5,29},{6,30},{7,31},{8,16},{9,... | collective-permute-start | bytes 36872 | tf_op jit(solution)/shard_map/ppermute | solution.py:445
  55.1 4.6 %collective-permute-start.14 = (f32[24,128]{1,0:T(8,128)S(1)}, f32[24,128]{1,0:T(8,128)S(1)}, u32[]{:S(2)}, u32[]{:S(2)}) collective-permute-start(f32[24,128]{1,0:T(8,128)S(1)} %get-tuple-element.97.refs_0_), channel_id=1, source_target_pairs={{0,16},{1,17},{2,18},{3,19},{4,20},{5,21},{6,22},{7,23},{8,24},{9,... | collective-permute-start | bytes 36872 | tf_op jit(solution)/shard_map/ppermute | solution.py:445
  55.1 4.6 %collective-permute-start.13 = (f32[24,128]{1,0:T(8,128)S(1)}, f32[24,128]{1,0:T(8,128)S(1)}, u32[]{:S(2)}, u32[]{:S(2)}) collective-permute-start(f32[24,128]{1,0:T(8,128)S(1)} %get-tuple-element.97.refs_0_), channel_id=1, source_target_pairs={{0,8},{1,9},{2,10},{3,11},{4,12},{5,13},{6,14},{7,15},{8,0},{9,1},... | collective-permute-start | bytes 36872 | tf_op jit(solution)/shard_map/ppermute | solution.py:445
